TPU v7x, 256 devices: a whole 4x4x8 slice. The times are simulated.
256 devices in a mesh: blk: 32 (over z_lo, y, core), row: 8 (over z_hi, x).
Axes of the slice: x: 4, y: 4, z: 8 (z_hi: 2, z_lo: 4; z = z_hi * 4 + z_lo), core: 2. Of those that a mesh axis runs over, the one named last changes fastest.
Arguments:
- features: float32 [16384, 256], P(('blk', 'row')), may hold values from -2 to 2, as said below
- probes: float32 [16384, 128], P(('blk', 'row')), may hold values from -6 to 6
- outputscale: float32 [1], replicated, may hold values from 0.05 to 0.2
- noise: float32 [1], replicated, may hold values from 0.5 to 2
- pivots: int32 [256], replicated, may hold values from 0 to 16383, as said below
Outputs:
- product: float32 [16384, 128], P(('blk', 'row'))
- preconditioned: float32 [16384, 128], P(('blk', 'row'))
Inputs may be any that keep to these rules, and one draw needn't show every extreme that they name: `pivots`: 256 distinct point indices. real-valued features.
All inputs are finite; a program needn't handle non-finite values.
Results may differ from a plain program's by a relative error of at most 0.0003.
Values sent between devices are 32-bit elements; how exact they have to be, the bound alone decides.
A program may use at most 64 MiB of HBM per device.

v0:
```python
import jax
import jax.numpy as jnp
from jax import lax
from jax.sharding import PartitionSpec as P

STRIDE = 4


highest = lax.Precision.HIGHEST
root_five = 2.23606797749979


def in_one_piece(arrays, axis, dim, along):
    widths = [a.shape[along] for a in arrays]
    both = jnp.concatenate(arrays, axis=along)
    result = lax.all_gather(both, axis, axis=dim, tiled=True)
    return tuple(jnp.split(result, [sum(widths[:k]) for k in range(1, len(widths))], axis=along))


def shifted(block, axis, distance):
    devices = range(lax.axis_size(axis))
    route = [((i - distance) % len(devices), i) for i in devices]
    return lax.ppermute(block, axis, route)


def in_blocks(x, dim, count):
    dims = x.shape
    tiles = x.reshape(*dims[:dim], count, dims[dim] // count, *dims[dim + 1 :])
    return jnp.moveaxis(tiles, dim, 0)


def sent_and_summed(x, axis, dim):
    count = lax.axis_size(axis)
    tiles = lax.all_to_all(in_blocks(x, dim, count), axis, 0, 0, tiled=True)
    return jnp.sum(tiles, axis=0)


def kernel_tile(row_feats, row_norms, col_feats, col_norms):
    inner = lax.dot_general(
        row_feats,
        col_feats,
        (((1,), (1,)), ((), ())),
        precision=highest,
        preferred_element_type=jnp.float32,
    )
    squared = jnp.maximum(row_norms[:, None] + col_norms[None, :] - 2.0 * inner, 0.0)
    scaled = root_five * jnp.sqrt(squared)
    return (1.0 + scaled + scaled * scaled / 3.0) * jnp.exp(-scaled)


def transposed_product(kernel_block, row_probes):
    return lax.dot_general(
        kernel_block,
        row_probes,
        (((0,), (0,)), ((), ())),
        precision=highest,
        preferred_element_type=jnp.float32,
    )


def quorum_members(block_count, spacing):
    half_count = block_count // 2
    members = list(range(spacing))
    reached = 0
    while reached < half_count:
        reached = reached + spacing
        members.append(reached % block_count)
    return members


def quorum_pairs(block_count, members):
    pair_list = []
    for offset in range(block_count // 2 + 1):
        chosen = None
        for lower_slot, lower_member in enumerate(members):
            for upper_slot, upper_member in enumerate(members):
                if chosen is None and (upper_member - lower_member) % block_count == offset:
                    chosen = (lower_slot, upper_slot)
        two_sided = offset != 0 and 2 * offset != block_count
        pair_list.append((chosen[0], chosen[1], two_sided))
    return pair_list


def per_device(features, probes, outputscale, noise, pivots):
    local_rows, probe_count = probes.shape
    block_count = lax.axis_size("blk")
    piece_count = lax.axis_size("row")
    piece_index = lax.axis_index("row")
    amplitude = outputscale[0]
    nugget = noise[0]
    members = quorum_members(block_count, STRIDE)
    pair_list = quorum_pairs(block_count, members)
    slot_count = len(members)
    block_rows = local_rows * piece_count
    own_norms = jnp.sum(features * features, axis=1)
    forward = [jnp.zeros((local_rows, probe_count), jnp.float32) for member in members]
    backward = [jnp.zeros((block_rows, probe_count), jnp.float32) for member in members]
    whole_feats, whole_probes = in_one_piece((features, probes), "row", 0, 1)
    fetched = [(whole_feats, whole_probes)]
    for member in members[1:]:
        fetched.append(shifted((whole_feats, whole_probes), "blk", block_count - member))
    fetched_norms = [jnp.sum(entry[0] * entry[0], axis=1) for entry in fetched]
    first_row = piece_index * local_rows
    for lower, upper, two_sided in pair_list:
        row_feats = lax.dynamic_slice_in_dim(fetched[lower][0], first_row, local_rows, 0)
        row_probes = lax.dynamic_slice_in_dim(fetched[lower][1], first_row, local_rows, 0)
        row_norms = lax.dynamic_slice_in_dim(fetched_norms[lower], first_row, local_rows, 0)
        kernel_block = kernel_tile(row_feats, row_norms, fetched[upper][0], fetched_norms[upper])
        forward[lower] = forward[lower] + jnp.dot(
            kernel_block, fetched[upper][1], precision=highest, preferred_element_type=jnp.float32
        )
        if two_sided:
            backward[upper] = backward[upper] + transposed_product(kernel_block, row_probes)
    shared = sent_and_summed(jnp.stack(backward), "row", 1)
    kernel_probes = forward[0] + shared[0]
    for position in range(1, slot_count):
        outgoing = forward[position] + shared[position]
        kernel_probes = kernel_probes + shifted(outgoing, "blk", members[position])
    product = amplitude * kernel_probes + nugget * probes
    flat_index = lax.axis_index("blk") * piece_count + piece_index
    offsets = pivots - flat_index * local_rows
    inside = (offsets >= 0) & (offsets < local_rows)
    picked = jnp.where(inside[:, None], features[jnp.clip(offsets, 0, local_rows - 1)], 0.0)
    pivot_feats = lax.psum(picked, ("blk", "row"))
    pivot_norms = jnp.sum(pivot_feats * pivot_feats, axis=1)
    cross = amplitude * kernel_tile(features, own_norms, pivot_feats, pivot_norms)
    gram_part = lax.dot_general(
        cross,
        cross,
        (((0,), (0,)), ((), ())),
        precision=highest,
        preferred_element_type=jnp.float32,
    )
    projected_part = lax.dot_general(
        cross,
        product,
        (((0,), (0,)), ((), ())),
        precision=highest,
        preferred_element_type=jnp.float32,
    )
    gram_sum, projected = lax.psum((gram_part, projected_part), ("blk", "row"))
    inner_pivots = amplitude * kernel_tile(pivot_feats, pivot_norms, pivot_feats, pivot_norms)
    gram = nugget * inner_pivots + gram_sum
    factor = jnp.linalg.cholesky(gram)
    coefficients = jax.scipy.linalg.cho_solve((factor, True), projected)
    preconditioned = (
        product
        - jnp.dot(cross, coefficients, precision=highest, preferred_element_type=jnp.float32)
    ) / nugget
    return (product, preconditioned)


def solution(mesh):
    in_specs = (P(("blk", "row"), None), P(("blk", "row"), None), P(), P(), P())
    out_specs = (P(("blk", "row"), None), P(("blk", "row"), None))
    return jax.shard_map(
        per_device, mesh=mesh, in_specs=in_specs, out_specs=out_specs, check_vma=False
    )
```

profile of v0, /device:TPU:1, one launch (start us, length us, event | category | flops | bytes accessed | tf_op | source)
XLA Modules:
  0.0 732.2 jit_solution(11525379217456375764)
XLA Ops:
  8.1 43.4 %all_gather.3 = f32[512,384]{1,0:T(8,128)S(1)} all-gather(f32[64,384]{1,0:T(8,128)S(1)} %pad_maximum_fusion), channel_id=1, replica_groups=mesh['blk'=32,'row'=8] {'row'}, dimensions={0}, use_global_device_ids=true | all-gather | bytes 884736 | tf_op jit(solution)/shard_map/all_gather | solution.py:16
  59.9 4.2 collective-permute-start.10
  67.3 18.6 %collective-permute-done.10 = f32[512,256]{1,0:T(8,128)S(1)} collective-permute-done((f32[512,256]{1,0:T(8,128)S(1)}, f32[512,256]{1,0:T(8,128)S(1)}, u32[]{:S(2)}, u32[]{:S(2)}) %collective-permute-start.10) | collective-permute-done | bytes 524320 | tf_op jit(solution)/shard_map/ppermute | solution.py:23
  89.2 44.4 %collective-permute-done.8 = f32[512,256]{1,0:T(8,128)S(1)} collective-permute-done((f32[512,256]{1,0:T(8,128)S(1)}, f32[512,256]{1,0:T(8,128)S(1)}, u32[]{:S(2)}, u32[]{:S(2)}) %collective-permute-start.8) | collective-permute-done | bytes 524320 | tf_op jit(solution)/shard_map/ppermute | solution.py:23
  133.5 8.1 %collective-permute-start.6 = (f32[512,256]{1,0:T(8,128)S(1)}, f32[512,256]{1,0:T(8,128)S(1)}, u32[]{:S(2)}, u32[]{:S(2)}) collective-permute-start(f32[512,256]{1,0:T(8,128)S(1)} %get-tuple-element.31), channel_id=1, source_target_pairs={{32,0},{40,8},{48,16},{56,24},{64,32},{72,40},{80,48},{88,56},{96,... | collective-permute-start | bytes 1572872 | tf_op jit(solution)/shard_map/ppermute | solution.py:23
  143.9 6.3 collective-permute-done.6
  150.3 10.8 %collective-permute-start.4 = (f32[512,256]{1,0:T(8,128)S(1)}, f32[512,256]{1,0:T(8,128)S(1)}, u32[]{:S(2)}, u32[]{:S(2)}) collective-permute-start(f32[512,256]{1,0:T(8,128)S(1)} %get-tuple-element.31), channel_id=1, source_target_pairs={{24,0},{32,8},{40,16},{48,24},{56,32},{64,40},{72,48},{80,56},{88,... | collective-permute-start | bytes 1572872 | tf_op jit(solution)/shard_map/ppermute | solution.py:23
  163.3 6.6 collective-permute-done.4
  174.5 7.5 %collective-permute-done.2 = f32[512,256]{1,0:T(8,128)S(1)} collective-permute-done((f32[512,256]{1,0:T(8,128)S(1)}, f32[512,256]{1,0:T(8,128)S(1)}, u32[]{:S(2)}, u32[]{:S(2)}) %collective-permute-start.2) | collective-permute-done | bytes 524320 | tf_op jit(solution)/shard_map/ppermute | solution.py:23
  186.7 4.3 collective-permute-done
  191.0 6.5 collective-permute-start.3
  206.6 3.7 collective-permute-done.1
  210.3 4.4 collective-permute-start.5
  219.2 10.6 %collective-permute-start.12 = (f32[512,256]{1,0:T(8,128)S(1)}, f32[512,256]{1,0:T(8,128)S(1)}, u32[]{:S(2)}, u32[]{:S(2)}) collective-permute-start(f32[512,256]{1,0:T(8,128)S(1)} %get-tuple-element.31), channel_id=1, source_target_pairs={{128,0},{136,8},{144,16},{152,24},{160,32},{168,40},{176,48},{184,... | collective-permute-start | bytes 1572872 | tf_op jit(solution)/shard_map/ppermute | solution.py:23
  231.1 17.6 %collective-permute-done.12 = f32[512,256]{1,0:T(8,128)S(1)} collective-permute-done((f32[512,256]{1,0:T(8,128)S(1)}, f32[512,256]{1,0:T(8,128)S(1)}, u32[]{:S(2)}, u32[]{:S(2)}) %collective-permute-start.12) | collective-permute-done | bytes 524320 | tf_op jit(solution)/shard_map/ppermute | solution.py:23
  254.2 9.1 %all-to-all-start = ((f32[8,8,64,128]{3,2,1,0:T(8,128)}), f32[8,8,64,128]{3,2,1,0:T(8,128)S(1)}, u32[]{:S(2)}, u32[]{:S(2)}) async-start(f32[8,8,64,128]{3,2,1,0:T(8,128)} %bitcast.172), calls=%async_computation | async-start | bytes 4194304 | tf_op jit(solution)/shard_map/all_to_all | solution.py:34
  266.7 100.5 %all-reduce.5.cloned.1.call-done = f32[256,256]{0,1:T(8,128)} async-done(((f32[256,256]{0,1:T(8,128)}), f32[256,256]{0,1:T(8,128)}) %all-reduce.5.cloned.1.call-update) | async-done | bytes 262160 | tf_op jit(solution)/shard_map/psum | solution.py:124
  399.2 4.2 collective-permute-start.20
  412.9 247.2 %all-reduce.7.cloned.1.call-done = (f32[256,128]{1,0:T(8,128)}, f32[256,256]{0,1:T(8,128)}) async-done(((f32[256,128]{1,0:T(8,128)}, f32[256,256]{0,1:T(8,128)}), (f32[256,128]{1,0:T(8,128)}, f32[256,256]{0,1:T(8,128)})) %all-reduce.7.cloned.1.call-update) | async-done | bytes 393232 | tf_op jit(solution)/shard_map/psum | solution.py:141
  662.0 11.7 %cholesky.49 = f32[128,128]{1,0:T(8,128)S(1)} custom-call(f32[128,128]{1,0:T(8,128)S(1)} %cholesky.115), custom_call_target="Cholesky" | custom-call | tf_op jit(solution)/shard_map/jit(cholesky)/cholesky | solution.py:144
  673.8 9.8 %custom-call.18 = f32[1,128,128]{1,2,0:T(8,128)S(1)} custom-call(f32[1,128,128]{2,1,0:T(8,128)S(1)} %get-tuple-element.37), custom_call_target="InvertDiagBlocksLowerTriangular" | custom-call | tf_op jit(solution)/shard_map/jit(cholesky)/cholesky | solution.py:144
  684.2 11.7 %cholesky.103 = f32[128,128]{1,0:T(8,128)S(1)} custom-call(f32[128,128]{1,0:T(8,128)S(1)} %convolution_subtract_fusion.2), custom_call_target="Cholesky" | custom-call | tf_op jit(solution)/shard_map/jit(cholesky)/cholesky | solution.py:144
  698.6 4.3 while.1
  702.9 19.7 %custom-call.19 = f32[2,128,128]{1,2,0:T(8,128)S(1)} custom-call(f32[2,128,128]{2,1,0:T(8,128)S(1)} %get-tuple-element.9), custom_call_target="InvertDiagBlocksLowerTriangular" | custom-call | tf_op jit(solution)/shard_map/jit(_cho_solve)/triangular_solve | solution.py:145
  (230 shorter events, 103.2 us)
Async XLA Ops:
  7.2 360.0 %all-reduce.5.cloned.1.call-start = ((), (), s32[]{:S(2)}) async-start(), calls=%async_computation.1 | async-start | bytes 524288 | tf_op jit(solution)/shard_map/psum | solution.py:124
  52.3 326.1 %collective-permute-start.13 = (f32[512,128]{1,0:T(8,128)}, f32[512,128]{1,0:T(8,128)}, u32[]{:S(2)}, u32[]{:S(2)}) collective-permute-start(f32[512,128]{1,0:T(8,128)} %split.9), channel_id=1, source_target_pairs={{128,0},{136,8},{144,16},{152,24},{160,32},{168,40},{176,48},{184,... | collective-permute-start | bytes 786440 | tf_op jit(solution)/shard_map/ppermute | solution.py:23
  55.7 317.0 %collective-permute-start.11 = (f32[512,128]{1,0:T(8,128)}, f32[512,128]{1,0:T(8,128)}, u32[]{:S(2)}, u32[]{:S(2)}) collective-permute-start(f32[512,128]{1,0:T(8,128)} %split.9), channel_id=1, source_target_pairs={{96,0},{104,8},{112,16},{120,24},{128,32},{136,40},{144,48},{152,5... | collective-permute-start | bytes 786440 | tf_op jit(solution)/shard_map/ppermute | solution.py:23
  58.3 327.4 %collective-permute-start.9 = (f32[512,128]{1,0:T(8,128)}, f32[512,128]{1,0:T(8,128)S(1)}, u32[]{:S(2)}, u32[]{:S(2)}) collective-permute-start(f32[512,128]{1,0:T(8,128)} %split.9), channel_id=1, source_target_pairs={{64,0},{72,8},{80,16},{88,24},{96,32},{104,40},{112,48},{120,56},{... | collective-permute-start | bytes 786440 | tf_op jit(solution)/shard_map/ppermute | solution.py:23
  59.6 339.5 %collective-permute-start.7 = (f32[512,128]{1,0:T(8,128)}, f32[512,128]{1,0:T(8,128)}, u32[]{:S(2)}, u32[]{:S(2)}) collective-permute-start(f32[512,128]{1,0:T(8,128)} %split.9), channel_id=1, source_target_pairs={{32,0},{40,8},{48,16},{56,24},{64,32},{72,40},{80,48},{88,56},{96,... | collective-permute-start | bytes 786440 | tf_op jit(solution)/shard_map/ppermute | solution.py:23
  59.9 26.0 %collective-permute-start.10 = (f32[512,256]{1,0:T(8,128)S(1)}, f32[512,256]{1,0:T(8,128)S(1)}, u32[]{:S(2)}, u32[]{:S(2)}) collective-permute-start(f32[512,256]{1,0:T(8,128)S(1)} %get-tuple-element.31), channel_id=1, source_target_pairs={{96,0},{104,8},{112,16},{120,24},{128,32},{136,40},{144,48},{152,5... | collective-permute-start | bytes 1572872 | tf_op jit(solution)/shard_map/ppermute | solution.py:23
  85.9 47.6 %collective-permute-start.8 = (f32[512,256]{1,0:T(8,128)S(1)}, f32[512,256]{1,0:T(8,128)S(1)}, u32[]{:S(2)}, u32[]{:S(2)}) collective-permute-start(f32[512,256]{1,0:T(8,128)S(1)} %get-tuple-element.31), channel_id=1, source_target_pairs={{64,0},{72,8},{80,16},{88,24},{96,32},{104,40},{112,48},{120,56},{... | collective-permute-start | bytes 1572872 | tf_op jit(solution)/shard_map/ppermute | solution.py:23
  133.5 16.7 %collective-permute-start.6 = (f32[512,256]{1,0:T(8,128)S(1)}, f32[512,256]{1,0:T(8,128)S(1)}, u32[]{:S(2)}, u32[]{:S(2)}) collective-permute-start(f32[512,256]{1,0:T(8,128)S(1)} %get-tuple-element.31), channel_id=1, source_target_pairs={{32,0},{40,8},{48,16},{56,24},{64,32},{72,40},{80,48},{88,56},{96,... | collective-permute-start | bytes 1572872 | tf_op jit(solution)/shard_map/ppermute | solution.py:23
  150.3 19.7 %collective-permute-start.4 = (f32[512,256]{1,0:T(8,128)S(1)}, f32[512,256]{1,0:T(8,128)S(1)}, u32[]{:S(2)}, u32[]{:S(2)}) collective-permute-start(f32[512,256]{1,0:T(8,128)S(1)} %get-tuple-element.31), channel_id=1, source_target_pairs={{24,0},{32,8},{40,16},{48,24},{56,32},{64,40},{72,48},{80,56},{88,... | collective-permute-start | bytes 1572872 | tf_op jit(solution)/shard_map/ppermute | solution.py:23
  169.9 12.0 %collective-permute-start.2 = (f32[512,256]{1,0:T(8,128)S(1)}, f32[512,256]{1,0:T(8,128)S(1)}, u32[]{:S(2)}, u32[]{:S(2)}) collective-permute-start(f32[512,256]{1,0:T(8,128)S(1)} %get-tuple-element.31), channel_id=1, source_target_pairs={{16,0},{24,8},{32,16},{40,24},{48,32},{56,40},{64,48},{72,56},{80,... | collective-permute-start | bytes 1572872 | tf_op jit(solution)/shard_map/ppermute | solution.py:23
  181.9 9.0 %collective-permute-start = (f32[512,256]{1,0:T(8,128)S(1)}, f32[512,256]{1,0:T(8,128)S(1)}, u32[]{:S(2)}, u32[]{:S(2)}) collective-permute-start(f32[512,256]{1,0:T(8,128)S(1)} %get-tuple-element.31), channel_id=1, source_target_pairs={{8,0},{16,8},{24,16},{32,24},{40,32},{48,40},{56,48},{64,56},{72,6... | collective-permute-start | bytes 1572872 | tf_op jit(solution)/shard_map/ppermute | solution.py:23
  191.0 12.9 %collective-permute-start.3 = (f32[512,128]{1,0:T(8,128)}, f32[512,128]{1,0:T(8,128)S(1)}, u32[]{:S(2)}, u32[]{:S(2)}) collective-permute-start(f32[512,128]{1,0:T(8,128)} %split.9), channel_id=1, source_target_pairs={{16,0},{24,8},{32,16},{40,24},{48,32},{56,40},{64,48},{72,56},{80,... | collective-permute-start | bytes 786440 | tf_op jit(solution)/shard_map/ppermute | solution.py:23
  203.9 6.3 collective-permute-start.1
  210.3 8.9 %collective-permute-start.5 = (f32[512,128]{1,0:T(8,128)}, f32[512,128]{1,0:T(8,128)S(1)}, u32[]{:S(2)}, u32[]{:S(2)}) collective-permute-start(f32[512,128]{1,0:T(8,128)} %split.9), channel_id=1, source_target_pairs={{24,0},{32,8},{40,16},{48,24},{56,32},{64,40},{72,48},{80,56},{88,... | collective-permute-start | bytes 786440 | tf_op jit(solution)/shard_map/ppermute | solution.py:23
  219.2 29.5 %collective-permute-start.12 = (f32[512,256]{1,0:T(8,128)S(1)}, f32[512,256]{1,0:T(8,128)S(1)}, u32[]{:S(2)}, u32[]{:S(2)}) collective-permute-start(f32[512,256]{1,0:T(8,128)S(1)} %get-tuple-element.31), channel_id=1, source_target_pairs={{128,0},{136,8},{144,16},{152,24},{160,32},{168,40},{176,48},{184,... | collective-permute-start | bytes 1572872 | tf_op jit(solution)/shard_map/ppermute | solution.py:23
  254.2 135.3 %all-to-all-start = ((f32[8,8,64,128]{3,2,1,0:T(8,128)}), f32[8,8,64,128]{3,2,1,0:T(8,128)S(1)}, u32[]{:S(2)}, u32[]{:S(2)}) async-start(f32[8,8,64,128]{3,2,1,0:T(8,128)} %bitcast.172), calls=%async_computation | async-start | bytes 4194304 | tf_op jit(solution)/shard_map/all_to_all | solution.py:34
  263.3 396.8 %all-reduce.7.cloned.1.call-start = ((), (), s32[]{:S(2)}) async-start(), calls=%async_computation.2 | async-start | bytes 786432 | tf_op jit(solution)/shard_map/psum | solution.py:141
  391.0 12.5 %collective-permute-start.14 = (f32[64,128]{1,0:T(8,128)S(1)}, f32[64,128]{1,0:T(8,128)S(1)}, u32[]{:S(2)}, u32[]{:S(2)}) collective-permute-start(f32[64,128]{1,0:T(8,128)S(1)} %fusion.24), channel_id=1, source_target_pairs={{248,0},{0,8},{8,16},{16,24},{24,32},{32,40},{40,48},{48,56},{56,6... | collective-permute-start | bytes 98312 | tf_op jit(solution)/shard_map/ppermute | solution.py:23
  395.2 9.9 %collective-permute-start.15 = (f32[64,128]{1,0:T(8,128)S(1)}, f32[64,128]{1,0:T(8,128)S(1)}, u32[]{:S(2)}, u32[]{:S(2)}) collective-permute-start(f32[64,128]{1,0:T(8,128)S(1)} %fusion.22), channel_id=1, source_target_pairs={{240,0},{248,8},{0,16},{8,24},{16,32},{24,40},{32,48},{40,56},{48,... | collective-permute-start | bytes 98312 | tf_op jit(solution)/shard_map/ppermute | solution.py:23
  397.6 9.8 %collective-permute-start.16 = (f32[64,128]{1,0:T(8,128)S(1)}, f32[64,128]{1,0:T(8,128)S(1)}, u32[]{:S(2)}, u32[]{:S(2)}) collective-permute-start(f32[64,128]{1,0:T(8,128)S(1)} %fusion.20), channel_id=1, source_target_pairs={{232,0},{240,8},{248,16},{0,24},{8,32},{16,40},{24,48},{32,56},{40... | collective-permute-start | bytes 98312 | tf_op jit(solution)/shard_map/ppermute | solution.py:23
  399.2 8.2 %collective-permute-start.17 = (f32[64,128]{1,0:T(8,128)S(1)}, f32[64,128]{1,0:T(8,128)S(1)}, u32[]{:S(2)}, u32[]{:S(2)}) collective-permute-start(f32[64,128]{1,0:T(8,128)S(1)} %get-tuple-element.32), channel_id=1, source_target_pairs={{224,0},{232,8},{240,16},{248,24},{0,32},{8,40},{16,48},{24,56},{3... | collective-permute-start | bytes 98312 | tf_op jit(solution)/shard_map/ppermute | solution.py:23
  399.2 8.2 %collective-permute-start.20 = (f32[64,128]{1,0:T(8,128)S(1)}, f32[64,128]{1,0:T(8,128)S(1)}, u32[]{:S(2)}, u32[]{:S(2)}) collective-permute-start(f32[64,128]{1,0:T(8,128)S(1)} %get-tuple-element.33), channel_id=1, source_target_pairs={{128,0},{136,8},{144,16},{152,24},{160,32},{168,40},{176,48},{184,... | collective-permute-start | bytes 98312 | tf_op jit(solution)/shard_map/ppermute | solution.py:23
  403.4 6.1 collective-permute-start.19
  405.1 5.4 collective-permute-start.18
  (39 other events, 1256.0 us)
Sparse Core Ops, SparseCore 0:
  66.1 301.1 all-reduce.4
  413.0 247.0 all-reduce.6
where the time goes:
time: 742 us; the launch traced here: 732 us
  waiting for transfers between devices  464 us (63%)
  starting transfers between devices  80.4 us (11%)
  matrix products  59.9 us (8%)
  other arithmetic  57.9 us (8%)
  blocking collectives  43.4 us (6%)
  between operations  18.1 us (2%)
  local copies, waits for them, and re-layouts  8.85 us (1%)
    psum x1, waiting for transfers between devices, per_device(): gram_sum, projected = lax.psum((gram_part, projected_part), ('blk', 'row'))  247 us
    ppermute x21, waiting for transfers between devices, shifted(): return lax.ppermute(block, axis, route)  116 us
    psum x1, waiting for transfers between devices, per_device(): pivot_feats = lax.psum(picked, ('blk', 'row'))  101 us
    ppermute x21, starting transfers between devices, shifted(): return lax.ppermute(block, axis, route)  71.3 us
    all_gather x1, blocking collectives, in_one_piece(): result = lax.all_gather(both, axis, axis=dim, tiled=True)  43.4 us
    another operation x6, other arithmetic, per_device(): factor = jnp.linalg.cholesky(gram)  34 us
    dot_general x17, matrix products, per_device(): jnp.dot(kernel_block, fetched[upper][1], precision=highest, preferred_ele...  25.9 us
    another operation x3, other arithmetic, per_device(): coefficients = jax.scipy.linalg.cho_solve((factor, True), projected)  19.7 us
  transfers between devices with their start and end apart: 24, of which 14 were waited for; matrix products, arithmetic and copies ran while one was open for 8% of the time, Pallas kernels for 0%

commit v1 on v0

v1 whole, which is shorter than its diff:
```python
import functools

import jax
import jax.numpy as jnp
from jax import lax
from jax.experimental import pallas as pl
from jax.experimental.pallas import tpu as pltpu
from jax.sharding import PartitionSpec as P

MESH = pl.DeviceIdType.MESH
highest = lax.Precision.HIGHEST
root_five = 2.23606797749979
f32 = jnp.float32
bf16 = jnp.bfloat16

NX, NY, NZ, NC = 4, 4, 8, 2
ZLO = 4
PLANE = NX * NY
LINE = NZ * NC


def split(x):
    hi = x.astype(bf16)
    return hi, (x - hi.astype(f32)).astype(bf16)


def dot_nt(a, b):
    return lax.dot_general(a, b, (((1,), (1,)), ((), ())), preferred_element_type=f32)


def dot_nn(a, b):
    return jnp.dot(a, b, preferred_element_type=f32)


def matern(scaled_square):
    s = jnp.maximum(scaled_square, 1e-30)
    t = s * lax.rsqrt(s)
    return (1.0 + t + s * (1.0 / 3.0)) * jnp.exp(-t)


def row_norms(x):
    ones = jnp.ones((8, x.shape[1]), f32)
    return lax.dot_general(
        ones, x * x, (((1,), (1,)), ((), ())), precision=highest, preferred_element_type=f32
    )[0:1]


def column_norms(x):
    return jnp.broadcast_to(jnp.sum(x * x, axis=1, keepdims=True), (x.shape[0], 128))


def twice(x):
    return jnp.concatenate([x, x], axis=1)


def exchange_kernel(
    feats_ref, probes_ref, pivots_ref, amp_ref, noise_ref,
    product_ref, proj_ref, gram_ref, cross_ref,
    a_buf, b_buf, pick, p1_buf, p2_src, p2_buf, piv,
    r_cat, r_norm, r_norm_row, c_cat, c_norm_row, v_cat, part,
    piv_cat, piv_rcat, ct_hi, ct_lo, g_src, g_buf, gram, q_all, q1_buf, q_src, q_buf, q_out, prod_buf,
    a_sem, b_sem, p1_sem, p2_sem, p3_sem, g1_sem, g2_sem, r_sem, q1_sem, q2_sem, q3_sem,
):
    n_rows, n_feat = feats_ref.shape
    n_probe = probes_ref.shape[1]
    rank = pivots_ref.shape[0]
    chunk = rank // PLANE
    blk, row = lax.axis_index("blk"), lax.axis_index("row")
    core = lax.rem(blk, NC)
    y = lax.rem(lax.div(blk, NC), NY)
    x = lax.rem(row, NX)
    z = lax.div(row, NX) * ZLO + lax.div(blk, NC * NY)
    here = y * NX + x

    def plane(dx, dy):
        xx, yy = lax.rem(x + (dx + NX), NX), lax.rem(y + (dy + NY), NY)
        return ((lax.div(blk, NC * NY) * NY + yy) * NC + core, lax.div(row, NX) * NX + xx), yy * NX + xx

    def line(dz, dc):
        zz, cc = lax.rem(z + (dz + NZ), NZ), lax.rem(core + dc, NC)
        return ((lax.rem(zz, ZLO) * NY + y) * NC + cc, lax.div(zz, ZLO) * NX + x)

    plane_offsets = sorted(
        [(dx, dy) for dx in range(NX) for dy in range(NY) if dx or dy],
        key=lambda o: min(o[0], NX - o[0]) + min(o[1], NY - o[1]),
    )
    line_offsets = sorted(
        [(dz, dc) for dz in range(NZ) for dc in range(NC) if dz or dc],
        key=lambda o: min(o[0], NZ - o[0]),
    )

    def send(src, dst, sem, k, device):
        copy = pltpu.make_async_remote_copy(
            src_ref=src, dst_ref=dst, send_sem=sem.at[0, k], recv_sem=sem.at[1, k],
            device_id=device, device_id_type=MESH,
        )
        copy.start()
        return copy

    barrier = pltpu.get_barrier_semaphore()
    for dx, dy in plane_offsets:
        pl.semaphore_signal(barrier, inc=1, device_id=plane(dx, dy)[0], device_id_type=MESH)
    for dz, dc in line_offsets:
        pl.semaphore_signal(barrier, inc=1, device_id=line(dz, dc), device_id_type=MESH)

    amp, noise = amp_ref[0], noise_ref[0]
    own = feats_ref[...] * root_five
    a_buf[0] = own
    b_buf[0, :, :n_feat] = own
    b_buf[0, :, n_feat:] = probes_ref[...]
    first = (blk * (NX * NZ // ZLO) + row) * n_rows
    local = lax.broadcasted_iota(jnp.int32, (rank, n_rows), 1) + first
    onehot = (local == pivots_ref[:, :n_rows]).astype(f32)
    pick[...] = lax.dot_general(
        onehot, own, (((1,), (0,)), ((), ())), precision=highest, preferred_element_type=f32
    )
    pl.semaphore_wait(barrier, PLANE + LINE - 2)

    def mine(ref):
        return ref.at[pl.ds(pl.multiple_of(here * chunk, chunk), chunk)]

    def plane_scatter(src, dst, sem):
        copies = []
        for dx, dy in plane_offsets:
            device, there = plane(dx, dy)
            k = dy * NX + dx
            source = src.at[pl.ds(pl.multiple_of(there * chunk, chunk), chunk)]
            copies.append(send(source, dst.at[k], sem, k, device))
        return copies

    def plane_gather(ref, sem):
        copies = []
        for dx, dy in plane_offsets:
            k = dy * NX + dx
            copies.append(send(mine(ref), mine(ref), sem, k, plane(dx, dy)[0]))
        return copies

    def line_gather(src, dst, sem):
        copies = []
        for dz, dc in line_offsets:
            k = dz * NC + dc
            copies.append(send(src, dst.at[k], sem, k, line(dz, dc)))
        return copies

    def landed(copies):
        for c in copies:
            c.wait_recv()

    def summed(own_value, buf, count):
        total = own_value
        for k in range(1, count):
            total = total + buf[k]
        return total

    everything = []

    p1 = plane_scatter(pick, p1_buf, p1_sem)

    half = n_rows // 2
    right, left = line(1, 0), line(-1, 0)
    sibling = line(0, 1)

    def b_slot(dz, dc):
        return b_buf.at[dz * NC + dc]

    def b_send(dz_from, dz_to, device):
        return send(b_slot(dz_from, 0), b_slot(dz_to, 0), b_sem, dz_to * NC, device)

    def b_sibling(dz):
        return send(b_slot(dz, 0), b_slot(dz, 1), b_sem, dz * NC + 1, sibling)

    ring = {1: b_send(0, 1, right), 7: b_send(0, 7, left)}
    across = {0: b_sibling(0)}

    a_copies = []
    for dx, dy in plane_offsets:
        k = dy * NX + dx
        a_copies.append(send(a_buf.at[0], a_buf.at[k], a_sem, k, plane(dx, dy)[0]))

    landed(p1)
    p2_src[...] = summed(pick[pl.ds(pl.multiple_of(here * chunk, chunk), chunk), :], p1_buf, PLANE)
    p2 = line_gather(p2_src, p2_buf, p2_sem)

    def forward(step):
        ring[step].wait_recv()
        ring[8 - step].wait_recv()
        if step < 3:
            ring[step + 1] = b_send(step, step + 1, right)
            ring[7 - step] = b_send(8 - step, 7 - step, left)
        else:
            lower, upper = pl.ds(0, half), pl.ds(half, half)
            ring[4] = send(b_slot(3, 0).at[lower], b_slot(4, 0).at[lower], b_sem, 8, right)
            ring["4b"] = send(b_slot(5, 0).at[upper], b_slot(4, 0).at[upper], b_sem, LINE, left)
        across[step] = b_sibling(step)
        across[8 - step] = b_sibling(8 - step)

    forward(1)

    landed(p2)
    piv_rows = pl.ds(pl.multiple_of(here * chunk, chunk), chunk)
    piv[piv_rows, :] = summed(p2_src[...], p2_buf, LINE)
    p3 = plane_gather(piv, p3_sem)

    forward(2)

    landed(a_copies)

    for k in range(PLANE):
        rows = slice(k * n_rows, (k + 1) * n_rows)
        value = a_buf[k]
        hi, lo = split(value * -2.0)
        r_cat[rows, :n_feat] = hi
        r_cat[rows, n_feat:2 * n_feat] = hi
        r_cat[rows, 2 * n_feat:] = lo
        r_norm[rows, :] = column_norms(value)
    for k in range(0, PLANE, 4):
        value = a_buf[pl.ds(k, 4)].reshape(4 * n_rows, n_feat)
        r_norm_row[:, k * n_rows:(k + 4) * n_rows] = row_norms(value)

    part[...] = jnp.zeros_like(part)
    width = 4 * n_rows
    tile = 256

    def columns(slots):
        for i, (dz, dc) in enumerate(slots):
            rows = slice(i * n_rows, (i + 1) * n_rows)
            value = b_buf[dz * NC + dc, :, :n_feat]
            hi, lo = split(value)
            c_cat[rows, :n_feat] = hi
            c_cat[rows, n_feat:2 * n_feat] = lo
            c_cat[rows, 2 * n_feat:] = hi
            hi, lo = split(b_buf[dz * NC + dc, :, n_feat:])
            v_cat[rows, :n_probe] = hi
            v_cat[rows, n_probe:] = lo
            c_norm_row[:, rows] = row_norms(value)

        def body(i, carry):
            rows = pl.ds(pl.multiple_of(i * tile, tile), tile)
            s = dot_nt(r_cat[rows, :], c_cat[...])
            k = matern(s + twice(r_norm[rows, :]) + c_norm_row[...])
            hi, lo = split(k)
            both = dot_nn(hi, v_cat[...])
            last = dot_nn(lo, v_cat[:, :n_probe])
            part[rows, :] = part[rows, :] + (both[:, :n_probe] + both[:, n_probe:] + last)
            return carry

        lax.fori_loop(0, part.shape[0] // tile, body, 0)

    across[0].wait_recv()
    across[1].wait_recv()
    columns([(0, 0), (0, 1), (1, 0), (1, 1)])

    forward(3)

    landed(p3)
    pv = piv[...]
    hi, lo = split(pv)
    piv_cat[:, :n_feat] = hi
    piv_cat[:, n_feat:2 * n_feat] = lo
    piv_cat[:, 2 * n_feat:] = hi
    hi, lo = split(pv * -2.0)
    piv_rcat[:, :n_feat] = hi
    piv_rcat[:, n_feat:2 * n_feat] = hi
    piv_rcat[:, 2 * n_feat:] = lo
    piv_norm = column_norms(pv)
    piv_norm_row = row_norms(pv)
    for i in range(r_cat.shape[0] // tile):
        rows = slice(i * tile, (i + 1) * tile)
        s = dot_nt(piv_cat[...], r_cat[rows, :])
        ct = amp * matern(s + twice(piv_norm) + r_norm_row[:, rows])
        hi, lo = split(ct)
        ct_hi[:, rows] = hi
        ct_lo[:, rows] = lo
    g_hi, g_lo = ct_hi[piv_rows, :], ct_lo[piv_rows, :]
    g_src[...] = dot_nt(g_hi, ct_hi[...]) + dot_nt(g_hi, ct_lo[...]) + dot_nt(g_lo, ct_hi[...])
    g1 = line_gather(g_src, g_buf, g1_sem)

    s = dot_nt(r_cat[:n_rows, :], piv_cat[...])
    cross_ref[...] = amp * matern(s + twice(r_norm[:n_rows, :]) + piv_norm_row)

    across[2].wait_recv()
    across[7].wait_recv()
    columns([(7, 0), (7, 1), (2, 0), (2, 1)])

    landed(g1)
    gram[piv_rows, :] = summed(g_src[...], g_buf, LINE)
    g2 = plane_gather(gram, g2_sem)

    ring[4].wait_recv()
    ring["4b"].wait_recv()
    across[4] = b_sibling(4)

    across[6].wait_recv()
    across[3].wait_recv()
    columns([(6, 0), (6, 1), (3, 0), (3, 1)])
    across[5].wait_recv()
    across[4].wait_recv()
    columns([(5, 0), (5, 1), (4, 0), (4, 1)])

    part[...] = part[...] * amp
    part[:n_rows, :] = part[:n_rows, :] + noise * probes_ref[...]
    r_copies = []
    for dx, dy in plane_offsets:
        k = dy * NX + dx
        source = part.at[pl.ds(k * n_rows, n_rows)]
        r_copies.append(send(source, prod_buf.at[k], r_sem, k, plane(-dx, -dy)[0]))

    hi, lo = split(part[...])
    both = dot_nn(ct_hi[...], jnp.concatenate([hi, lo], axis=1))
    q_all[...] = both[:, :n_probe] + both[:, n_probe:] + dot_nn(ct_lo[...], hi)
    q1 = plane_scatter(q_all, q1_buf, q1_sem)
    landed(q1)
    q_src[...] = summed(q_all[piv_rows, :], q1_buf, PLANE)
    q2 = line_gather(q_src, q_buf, q2_sem)

    s = dot_nt(piv_rcat[...], piv_cat[...])
    inner = (noise * amp) * matern(s + twice(piv_norm) + piv_norm_row)

    landed(r_copies)
    product_ref[...] = summed(part[:n_rows, :], prod_buf, PLANE)

    landed(q2)
    q_out[piv_rows, :] = summed(q_src[...], q_buf, LINE)
    q3 = plane_gather(q_out, q3_sem)
    landed(g2)
    gram_ref[...] = gram[...] + inner
    landed(q3)
    proj_ref[...] = q_out[...]

    for group in (p1, p2, p3, g1, g2, q1, q2, q3, r_copies, a_copies, ring.values(), across.values()):
        for c in group:
            c.wait_send()


def per_device(features, probes, outputscale, noise, pivots):
    n_rows, n_feat = features.shape
    n_probe = probes.shape[1]
    rank = pivots.shape[0]
    chunk = rank // PLANE
    wide = PLANE * n_rows
    block = 4 * n_rows
    vmem = pltpu.VMEM
    dma = pltpu.SemaphoreType.DMA
    spread = jnp.broadcast_to(pivots[:, None], (rank, 128))
    product, projected, gram, cross = pl.pallas_call(
        exchange_kernel,
        out_shape=(
            jax.ShapeDtypeStruct((n_rows, n_probe), f32),
            jax.ShapeDtypeStruct((rank, n_probe), f32),
            jax.ShapeDtypeStruct((rank, rank), f32),
            jax.ShapeDtypeStruct((n_rows, rank), f32),
        ),
        in_specs=[pl.BlockSpec(memory_space=vmem)] * 3
        + [pl.BlockSpec(memory_space=pltpu.SMEM)] * 2,
        out_specs=[pl.BlockSpec(memory_space=vmem)] * 4,
        scratch_shapes=[
            vmem((PLANE, n_rows, n_feat), f32),
            vmem((LINE, n_rows, n_feat + n_probe), f32),
            vmem((rank, n_feat), f32),
            vmem((PLANE, chunk, n_feat), f32),
            vmem((chunk, n_feat), f32),
            vmem((LINE, chunk, n_feat), f32),
            vmem((rank, n_feat), f32),
            vmem((wide, 3 * n_feat), bf16),
            vmem((wide, 128), f32),
            vmem((1, wide), f32),
            vmem((block, 3 * n_feat), bf16),
            vmem((1, block), f32),
            vmem((block, 2 * n_probe), bf16),
            vmem((wide, n_probe), f32),
            vmem((rank, 3 * n_feat), bf16),
            vmem((rank, 3 * n_feat), bf16),
            vmem((rank, wide), bf16),
            vmem((rank, wide), bf16),
            vmem((chunk, rank), f32),
            vmem((LINE, chunk, rank), f32),
            vmem((rank, rank), f32),
            vmem((rank, n_probe), f32),
            vmem((PLANE, chunk, n_probe), f32),
            vmem((chunk, n_probe), f32),
            vmem((LINE, chunk, n_probe), f32),
            vmem((rank, n_probe), f32),
            vmem((PLANE, n_rows, n_probe), f32),
        ]
        + [dma((2, PLANE)), dma((2, LINE + 1)), dma((2, PLANE)), dma((2, LINE)), dma((2, PLANE))]
        + [dma((2, LINE)), dma((2, PLANE)), dma((2, PLANE)), dma((2, PLANE)), dma((2, LINE)), dma((2, PLANE))],
        compiler_params=pltpu.CompilerParams(
            collective_id=0, has_side_effects=True, vmem_limit_bytes=40 * 1024 * 1024
        ),
        name="exchange",
    )(features, probes, spread, outputscale, noise)
    nugget = noise[0]
    factor = jnp.linalg.cholesky(gram)
    coefficients = jax.scipy.linalg.cho_solve((factor, True), projected)
    preconditioned = (
        product - jnp.dot(cross, coefficients, precision=highest, preferred_element_type=f32)
    ) / nugget
    return product, preconditioned


def solution(mesh):
    in_specs = (P(("blk", "row"), None), P(("blk", "row"), None), P(), P(), P())
    out_specs = (P(("blk", "row"), None), P(("blk", "row"), None))
    return jax.shard_map(
        per_device, mesh=mesh, in_specs=in_specs, out_specs=out_specs, check_vma=False
    )
```

time: 742 us -> 141 us (0.19); the launches traced: 732 us -> 140 us
  waiting for transfers between devices: 464 us -> 0 us
  starting transfers between devices: 80.4 us -> 0 us
  Pallas kernels: 0 us -> 75.2 us
  matrix products: 59.9 us -> 2.78 us
  blocking collectives: 43.4 us -> 0 us
  between operations: 18.1 us -> 3.47 us
    psum x2 -> x0, waiting for transfers between devices: 348 us -> none  [the longest x1 247 us: per_device(): gram_sum, projected = lax.psum((gram_part, projected_part), ('blk', 'row'))]
    ppermute x21 -> x0, waiting for transfers between devices: 116 us -> none  [shifted(): return lax.ppermute(block, axis, route)]
    pallas_call x0 -> x1, Pallas kernels: none -> 75.2 us  [per_device(): pl.pallas_call(exchange_kernel, out_shape=(jax.ShapeDtypeStruct((n_rows,...]
    ppermute x21 -> x0, starting transfers between devices: 71.3 us -> none  [shifted(): return lax.ppermute(block, axis, route)]
    dot_general x54 -> x1, matrix products: 58 us -> 0.84 us  [per_device(): jnp.dot(cross, coefficients, precision=highest, preferred_element_type=f32)]
    all_gather x1 -> x0, blocking collectives: 43.4 us -> none  [in_one_piece(): result = lax.all_gather(both, axis, axis=dim, tiled=True)]
    all_to_all x1 -> x0, starting transfers between devices: 9.09 us -> none  [sent_and_summed(): tiles = lax.all_to_all(in_blocks(x, dim, count), axis, 0, 0, tiled=True)]
  transfers between devices with their start and end apart: 24 -> 0, of which waited for: 14 -> 0; matrix products, arithmetic and copies ran while one was open for 8% -> 0% of each run, Pallas kernels for 0% -> 0%
where the time goes in v1:
time: 141 us; the launch traced here: 140 us
  Pallas kernels  75.2 us (53%)
  other arithmetic  53.9 us (38%)
  local copies, waits for them, and re-layouts  5.04 us (4%)
  between operations  3.47 us (2%)
  matrix products  2.78 us (2%)
    pallas_call x1, Pallas kernels, per_device(): pl.pallas_call(exchange_kernel, out_shape=(jax.ShapeDtypeStruct((n_rows,...  75.2 us
    another operation x6, other arithmetic, per_device(): factor = jnp.linalg.cholesky(gram)  34.2 us
    another operation x3, other arithmetic, per_device(): coefficients = jax.scipy.linalg.cho_solve((factor, True), projected)  19.7 us
    another operation x6, local copies, waits for them, and re-layouts  4.02 us

profile of v1, /device:TPU:1, one launch (start us, length us, event | category | flops | bytes accessed | tf_op | source)
XLA Modules:
  0.0 140.4 jit_solution(12415528491995791048)
XLA Ops:
  1.3 0.1 broadcast_in_dim.3.pivots_ref
  2.2 75.2 %exchange.1 = (f32[64,128]{1,0:T(8,128)S(1)}, f32[256,128]{1,0:T(8,128)S(1)}, f32[256,256]{1,0:T(8,128)S(1)}, f32[64,256]{1,0:T(8,128)S(1)}) custom-call(f32[64,256]{1,0:T(8,128)S(1)} %copy-done, f32[64,128]{1,0:T(8,128)S(1)} %copy-done.1, s32[256,128]{1,0:T(8,128)S(1)} %broadcast_in_dim.3.pivots_ref, f32[1]{0:T(128)S(6)} %copy.19.amp_ref, f32[1]{0:T(128)} %copy.20.noise_ref), custom_call_target="tpu_custom_call" | custom-call | tf_op jit(solution)/shard_map/exchange/pallas_call | solution.py:345
  77.3 0.1 copy.7
  77.5 11.7 %cholesky.50 = f32[128,128]{1,0:T(8,128)S(1)} custom-call(f32[128,128]{1,0:T(8,128)S(1)} %cholesky.118), custom_call_target="Cholesky" | custom-call | tf_op jit(solution)/shard_map/jit(cholesky)/cholesky | solution.py:393
  89.3 9.8 %custom-call.18 = f32[1,128,128]{1,2,0:T(8,128)S(1)} custom-call(f32[1,128,128]{2,1,0:T(8,128)S(1)} %get-tuple-element.31), custom_call_target="InvertDiagBlocksLowerTriangular" | custom-call | tf_op jit(solution)/shard_map/jit(cholesky)/cholesky | solution.py:393
  99.1 0.2 constant_dynamic-update-slice_fusion.1
  99.3 0.3 convolution_subtract_fusion.2
  99.6 11.9 %cholesky.105 = f32[128,128]{1,0:T(8,128)S(1)} custom-call(f32[128,128]{1,0:T(8,128)S(1)} %convolution_subtract_fusion.2), custom_call_target="Cholesky" | custom-call | tf_op jit(solution)/shard_map/jit(cholesky)/cholesky | solution.py:393
  111.5 0.7 compare_reduce_fusion
  113.7 0.1 triangular_solve.66
  113.7 4.1 %while.1 = (s32[]{:T(128)}, f32[256,256]{1,0:T(8,128)S(1)}, s32[2,2]{1,0:T(2,128)S(1)}, f32[2,128,128]{2,1,0:T(8,128)S(1)}, s32[]{:T(128)}) while((s32[]{:T(128)}, f32[256,256]{1,0:T(8,128)S(1)}, s32[2,2]{1,0:T(2,128)S(1)}, f32[2,128,128]{2,1,0:T(8,128)S(1)}, s32[]{:T(128)}) %tuple.27), condition=%wide.while_cond, body=%wide.while_body.sunk | while | flops 2 | bytes 131181 | solution.py:394
  113.7 0.7 fusion.26
  114.4 1.3 bitcast_dynamic-update-slice_fusion.2
  115.8 0.7 fusion.26
  116.4 1.3 bitcast_dynamic-update-slice_fusion.2
  117.8 19.7 %custom-call.19 = f32[2,128,128]{1,2,0:T(8,128)S(1)} custom-call(f32[2,128,128]{2,1,0:T(8,128)S(1)} %get-tuple-element.17), custom_call_target="InvertDiagBlocksLowerTriangular" | custom-call | tf_op jit(solution)/shard_map/jit(_cho_solve)/triangular_solve | solution.py:394
  137.5 0.3 fusion.8
  137.8 0.2 convolution_subtract_fusion.1
  138.0 0.3 fusion.12
  138.3 0.2 fusion.11
  138.5 0.3 convolution_subtract_fusion
  138.8 0.2 fusion.10
  139.0 0.8 fusion
  139.8 0.6 copy.22
  (16 shorter events, 0.3 us)
Async XLA Ops:
  0.6 0.7 copy-start.2
  1.3 0.8 copy-start
  1.3 0.8 copy-start.1

commit v2 on v1

v2 whole, which is shorter than its diff:
```python
import jax
import jax.numpy as jnp
from jax import lax
from jax.experimental import pallas as pl
from jax.experimental.pallas import tpu as pltpu
from jax.sharding import PartitionSpec as P

MESH = pl.DeviceIdType.MESH
highest = lax.Precision.HIGHEST
root_five = 2.23606797749979
f32 = jnp.float32
bf16 = jnp.bfloat16

NX, NY, NZ, NC = 4, 4, 8, 2
ZLO = 4
PLANE = NX * NY
LINE = NZ * NC


def split(x):
    hi = x.astype(bf16)
    return hi, (x - hi.astype(f32)).astype(bf16)


def dot_nt(a, b):
    return lax.dot_general(a, b, (((1,), (1,)), ((), ())), preferred_element_type=f32)


def dot_nn(a, b):
    return jnp.dot(a, b, preferred_element_type=f32)


def matern(scaled_square):
    s = jnp.maximum(scaled_square, 1e-30)
    t = s * lax.rsqrt(s)
    return (1.0 + t + s * (1.0 / 3.0)) * jnp.exp(-t)


def column_norms(x):
    return jnp.broadcast_to(jnp.sum(x * x, axis=1, keepdims=True), (x.shape[0], 128))


def as_row(norms):
    return jnp.transpose(norms)[0:1]


def twice(x):
    return jnp.concatenate([x, x], axis=1)


def dot_exact(a, b):
    return jnp.dot(a, b, precision=highest, preferred_element_type=f32)


def invert(work, first_tile, last_tile):
    tiles, _, half = work.shape
    sub = lax.broadcasted_iota(jnp.int32, (8, half), 0)
    lane = lax.broadcasted_iota(jnp.int32, (8, half), 1)

    def spread_lane(v, index):
        return jnp.take_along_axis(v, index, axis=1)

    def spread_row(v, r):
        return jnp.broadcast_to(v[r:r + 1, :], v.shape)

    def reciprocal(d):
        r = pl.reciprocal(d, approx=True)
        r = r * (2.0 - d * r)
        return r * (2.0 - d * r)

    def step(kb, carry):
        start = kb * 8
        index = [jnp.full((8, half), start + c, jnp.int32) for c in range(8)]
        active = (lane >= start) & (lane < start + 8)
        top = work[kb]
        d = [spread_lane(top, index[c]) for c in range(8)]
        top = jnp.where(active, jnp.where(lane - start == sub, 1.0, 0.0), top)
        for s in range(0, 8, 2):
            a, b, c = spread_row(d[s], s), spread_row(d[s + 1], s), spread_row(d[s + 1], s + 1)
            inverse = reciprocal(a * c - b * b)
            a, b, c = a * inverse, b * inverse, c * inverse
            first, second = d[s], d[s + 1]

            def swept(v):
                r0, r1 = spread_row(v, s), spread_row(v, s + 1)
                p0 = c * r0 - b * r1
                p1 = a * r1 - b * r0
                rest = v - first * p0 - second * p1
                return jnp.where(sub == s, p0, jnp.where(sub == s + 1, p1, rest))

            for c2 in range(s + 2, 8):
                d[c2] = swept(d[c2])
            top = swept(top)
        rows = [spread_row(top, c) for c in range(8)]
        for r in range(tiles):
            v = work[r]
            total = jnp.where(active, 0.0, v)
            for c in range(8):
                total = total - spread_lane(v, index[c]) * rows[c]
            work[r] = total
        work[kb] = top
        return carry

    lax.fori_loop(first_tile, last_tile, step, 0)


def exchange_kernel(
    feats_ref, probes_ref, pivots_ref, amp_ref, noise_ref,
    product_ref, out_ref,
    a_buf, b_buf, pick, p_buf, piv,
    r_cat, r_norm, r_norm_row, c_cat, c_norm_row, v_cat, part,
    piv_cat, ct, ct_hi, ct_lo, cross_own, g_src, g_buf, gram, q_all, q1_buf, q_src, q_buf, q_out, prod_buf, work, full,
    a_sem, b_sem, p_sem, g_sem, q_sem, q1_sem, r_sem,
):
    n_rows, n_feat = feats_ref.shape
    n_probe = probes_ref.shape[1]
    rank = pivots_ref.shape[0]
    half_rank = rank // NC
    chunk = half_rank // PLANE
    half_feat = n_feat // 2
    blk, row = lax.axis_index("blk"), lax.axis_index("row")
    core = lax.rem(blk, NC)
    y = lax.rem(lax.div(blk, NC), NY)
    x = lax.rem(row, NX)
    z = lax.div(row, NX) * ZLO + lax.div(blk, NC * NY)
    here = y * NX + x

    def plane(dx, dy):
        xx, yy = lax.rem(x + (dx + NX), NX), lax.rem(y + (dy + NY), NY)
        return ((lax.div(blk, NC * NY) * NY + yy) * NC + core, lax.div(row, NX) * NX + xx), yy * NX + xx

    def line(dz, dc):
        zz, cc = lax.rem(z + (dz + NZ), NZ), lax.rem(core + dc, NC)
        return ((lax.rem(zz, ZLO) * NY + y) * NC + cc, lax.div(zz, ZLO) * NX + x), cc

    plane_offsets = sorted(
        [(dx, dy) for dx in range(NX) for dy in range(NY) if dx or dy],
        key=lambda o: -(min(o[0], NX - o[0]) + min(o[1], NY - o[1])),
    )
    line_offsets = sorted(
        [(dz, dc) for dz in range(NZ) for dc in range(NC) if dz or dc],
        key=lambda o: -min(o[0], NZ - o[0]),
    )

    everything = []

    def send(src, dst, sem, k, device):
        copy = pltpu.make_async_remote_copy(
            src_ref=src, dst_ref=dst, send_sem=sem.at[0, k], recv_sem=sem.at[1, k],
            device_id=device, device_id_type=MESH,
        )
        copy.start()
        everything.append(copy)
        return copy

    barrier = pltpu.get_barrier_semaphore()
    for dx, dy in plane_offsets:
        pl.semaphore_signal(barrier, inc=1, device_id=plane(dx, dy)[0], device_id_type=MESH)
    for dz, dc in line_offsets:
        pl.semaphore_signal(barrier, inc=1, device_id=line(dz, dc)[0], device_id_type=MESH)

    amp, noise = amp_ref[0], noise_ref[0]
    own = feats_ref[...] * root_five
    a_buf[0, 0, 0] = own[:, :half_feat]
    a_buf[1, 0, 0] = own[:, half_feat:]
    b_buf[0, :, :n_feat] = own
    b_buf[0, :, n_feat:] = probes_ref[...]
    pl.semaphore_wait(barrier, PLANE + LINE - 2)

    def landed(copies):
        for c in copies:
            c.wait_recv()

    upper_rows, lower_rows = pl.ds(0, n_rows // 2), pl.ds(n_rows // 2, n_rows // 2)

    moved = {}

    def a_slot(h, u, v):
        return a_buf.at[(h, v, u) if h == 0 else (h, u, v)]

    def a_send(h, u, v, du, dv, part_of=None):
        to = ((u + du) % 4, (v + dv) % 4)
        src, dst = a_slot(h, u, v), a_slot(h, *to)
        if part_of is not None:
            src, dst = src.at[part_of], dst.at[part_of]
        index = 2 * (16 * h + 4 * to[0] + to[1]) + (part_of is lower_rows)
        device = plane(du, dv)[0] if h == 0 else plane(dv, du)[0]
        moved[(h, *to, part_of is lower_rows)] = send(src, dst, a_sem, index, device)

    def a_wait(*slots):
        for u, v in slots:
            for h in range(2):
                for low in (False, True):
                    if (h, u, v, low) in moved:
                        moved[(h, u, v, low)].wait_recv()

    def a_round(step):
        for h in range(2):
            if step == 0:
                for d in (1, -1):
                    a_send(h, 0, 0, d, 0)
                    a_send(h, 0, 0, 0, d)
            if step == 1:
                a_send(h, 1, 0, 1, 0, upper_rows)
                a_send(h, 3, 0, -1, 0, lower_rows)
                for u in (1, 3):
                    for d in (1, -1):
                        a_send(h, u, 0, 0, d)
                a_send(h, 0, 1, 0, 1, upper_rows)
                a_send(h, 0, 3, 0, -1, lower_rows)
            if step == 2:
                for d in (1, -1):
                    a_send(h, 2, 0, 0, d)
                for u in (1, 3):
                    a_send(h, u, 1, 0, 1, upper_rows)
                    a_send(h, u, 3, 0, -1, lower_rows)
            if step == 3:
                a_send(h, 2, 1, 0, 1, upper_rows)
                a_send(h, 2, 3, 0, -1, lower_rows)

    right, left = line(1, 0)[0], line(-1, 0)[0]
    sibling = line(0, 1)[0]

    def b_slot(dz, dc):
        return b_buf.at[dz * NC + dc]

    def b_send(dz_from, dz_to, device):
        return send(b_slot(dz_from, 0), b_slot(dz_to, 0), b_sem, dz_to * NC, device)

    def b_sibling(dz):
        return send(b_slot(dz, 0), b_slot(dz, 1), b_sem, dz * NC + 1, sibling)

    def forward(step):
        ring[step].wait_recv()
        ring[8 - step].wait_recv()
        if step < 3:
            ring[step + 1] = b_send(step, step + 1, right)
            ring[7 - step] = b_send(8 - step, 7 - step, left)
        else:
            ring[4] = send(b_slot(3, 0).at[upper_rows], b_slot(4, 0).at[upper_rows], b_sem, 8, right)
            ring["4b"] = send(b_slot(5, 0).at[lower_rows], b_slot(4, 0).at[lower_rows], b_sem, LINE, left)
        across[step] = b_sibling(step)
        across[8 - step] = b_sibling(8 - step)

    def prepare(slots):
        for dx, dy in slots:
            k = dy * NX + dx
            rows = slice(k * n_rows, (k + 1) * n_rows)
            total = None
            for h in range(2):
                value = a_buf[h, dy, dx]
                hi, lo = split(value * -2.0)
                r_cat[rows, h * half_feat:(h + 1) * half_feat] = hi
                r_cat[rows, n_feat + h * half_feat:n_feat + (h + 1) * half_feat] = hi
                r_cat[rows, 2 * n_feat + h * half_feat:2 * n_feat + (h + 1) * half_feat] = lo
                square = value * value
                total = square if total is None else total + square
            r_norm[rows, :] = jnp.broadcast_to(jnp.sum(total, axis=1, keepdims=True), (n_rows, 128))

    a_round(0)
    ring = {1: b_send(0, 1, right), 7: b_send(0, 7, left)}
    across = {0: b_sibling(0)}
    prepare([(0, 0)])
    a_wait((1, 0), (3, 0), (0, 1), (0, 3))
    a_round(1)
    forward(1)
    prepare([(1, 0), (3, 0), (0, 1), (0, 3)])
    a_wait((2, 0), (1, 1), (1, 3), (3, 1), (3, 3))
    a_round(2)
    forward(2)
    a_wait((0, 2))
    prepare([(1, 1), (1, 3), (3, 1), (3, 3), (2, 0), (0, 2)])
    a_wait((2, 1), (2, 3))
    a_round(3)
    forward(3)
    a_wait((1, 2), (3, 2), (2, 2))
    prepare([(2, 1), (2, 3), (1, 2), (3, 2), (2, 2)])

    def my_rows(c):
        return pl.ds(pl.multiple_of(c * half_rank + here * chunk, chunk), chunk)

    position = lax.broadcasted_iota(jnp.int32, (8, PLANE * n_rows), 1)
    slot = position // n_rows
    from_x = (x + NX - slot % NX) % NX
    from_y = (y + NY - slot // NX) % NY
    point = (((z % ZLO * NY + from_y) * NC + core) * (NX * NZ // ZLO) + z // ZLO * NX + from_x) * n_rows
    point = point + position % n_rows
    onehot = []
    for c in range(NC):
        wanted = pivots_ref[my_rows(c), :]
        onehot.append((point == jnp.concatenate([wanted] * (PLANE * n_rows // 128), axis=1)).astype(f32))
    onehot = jnp.concatenate(onehot, axis=0)
    for h in range(2):
        value = dot_exact(onehot, a_buf[h].reshape(PLANE * n_rows, half_feat))
        pick[:, :, h * half_feat:(h + 1) * half_feat] = value.reshape(NC, chunk, half_feat)

    def line_reduce(src, dst, sem):
        copies = []
        for dz, dc in line_offsets:
            device, cc = line(dz, dc)
            k = dz * NC + dc
            copies.append(send(src.at[cc], dst.at[k], sem, k, device))
        return copies

    def plane_gather(ref, sem):
        copies = []
        for dx, dy in plane_offsets:
            mine = ref.at[my_rows(core)]
            copies.append(send(mine, mine, sem, LINE + dy * NX + dx, plane(dx, dy)[0]))
        return copies

    def sibling_gather(ref, sem):
        mine = ref.at[pl.ds(pl.multiple_of(core * half_rank, half_rank), half_rank)]
        return send(mine, mine, sem, LINE + PLANE, sibling)

    def summed(total, buf, count):
        for k in range(1, count):
            total = total + buf[k]
        return total

    p_line = line_reduce(pick, p_buf, p_sem)

    for k in range(0, r_norm.shape[0], 128):
        r_norm_row[:, k:k + 128] = as_row(r_norm[k:k + 128, :])
    part[...] = jnp.zeros_like(part)
    tile = 256

    def columns(slots):
        for i, (dz, dc) in enumerate(slots):
            rows = slice(i * n_rows, (i + 1) * n_rows)
            value = b_buf[dz * NC + dc, :, :n_feat]
            hi, lo = split(value)
            c_cat[rows, :n_feat] = hi
            c_cat[rows, n_feat:2 * n_feat] = lo
            c_cat[rows, 2 * n_feat:] = hi
            hi, lo = split(b_buf[dz * NC + dc, :, n_feat:])
            v_cat[rows, :n_probe] = hi
            v_cat[rows, n_probe:] = lo
        for i in range(0, len(slots), 2):
            pair = [column_norms(b_buf[dz * NC + dc, :, :n_feat]) for dz, dc in slots[i:i + 2]]
            c_norm_row[:, i * n_rows:(i + 2) * n_rows] = as_row(jnp.concatenate(pair, axis=0))

        def body(i, carry):
            rows = pl.ds(pl.multiple_of(i * tile, tile), tile)
            s = dot_nt(r_cat[rows, :], c_cat[...])
            k = matern(s + twice(r_norm[rows, :]) + c_norm_row[...])
            hi, lo = split(k)
            both = dot_nn(hi, v_cat[...])
            last = dot_nn(lo, v_cat[:, :n_probe])
            part[rows, :] = part[rows, :] + (both[:, :n_probe] + both[:, n_probe:] + last)
            return carry

        lax.fori_loop(0, part.shape[0] // tile, body, 0)

    across[0].wait_recv()
    across[1].wait_recv()
    columns([(0, 0), (0, 1), (1, 0), (1, 1)])

    landed(p_line)
    piv[my_rows(core), :] = summed(pick[core], p_buf, LINE)
    p_plane = plane_gather(piv, p_sem)
    ring[4].wait_recv()
    ring["4b"].wait_recv()
    across[4] = b_sibling(4)

    across[2].wait_recv()
    across[7].wait_recv()
    columns([(7, 0), (7, 1), (2, 0), (2, 1)])

    landed(p_plane)
    p_side = sibling_gather(piv, p_sem)
    across[6].wait_recv()
    across[3].wait_recv()
    columns([(6, 0), (6, 1), (3, 0), (3, 1)])

    p_side.wait_recv()
    pv = piv[...]
    hi, lo = split(pv)
    piv_cat[:, :n_feat] = hi
    piv_cat[:, n_feat:2 * n_feat] = lo
    piv_cat[:, 2 * n_feat:] = hi
    piv_norm = column_norms(pv)
    piv_norm_row = jnp.concatenate([as_row(piv_norm[k:k + 128]) for k in range(0, rank, 128)], axis=1)
    for i in range(r_cat.shape[0] // tile):
        rows = slice(i * tile, (i + 1) * tile)
        s = dot_nt(piv_cat[...], r_cat[rows, :])
        value = amp * matern(s + twice(piv_norm) + r_norm_row[:, rows])
        ct[:, rows] = value
        hi, lo = split(value)
        ct_hi[:, rows] = hi
        ct_lo[:, rows] = lo
    hi, lo = split(jnp.concatenate([ct[my_rows(c), :] for c in range(NC)], axis=0))
    both = dot_nt(jnp.concatenate([hi, lo], axis=0), ct_hi[...])
    g = both[:NC * chunk] + both[NC * chunk:] + dot_nt(hi, ct_lo[...])
    g_src[...] = g.reshape(NC, chunk, rank)
    g_line = line_reduce(g_src, g_buf, g_sem)

    s = dot_nt(r_cat[:n_rows, :], piv_cat[...])
    cross_own[...] = amp * matern(s + twice(r_norm[:n_rows, :]) + piv_norm_row)
    across[5].wait_recv()
    across[4].wait_recv()
    columns([(5, 0), (5, 1), (4, 0), (4, 1)])

    landed(g_line)
    gram[my_rows(core), :] = summed(g_src[core], g_buf, LINE)
    g_plane = plane_gather(gram, g_sem)

    part[...] = part[...] * amp
    part[:n_rows, :] = part[:n_rows, :] + noise * probes_ref[...]
    hi, lo = split(part[...])
    both = dot_nn(ct_hi[...], jnp.concatenate([hi, lo], axis=1))
    q = both[:, :n_probe] + both[:, n_probe:] + dot_nn(ct_lo[...], hi)
    q_all[...] = q.reshape(NC, PLANE, chunk, n_probe)
    q1 = []
    for dx, dy in plane_offsets:
        device, there = plane(dx, dy)
        k = dy * NX + dx
        q1.append(send(q_all.at[:, there], q1_buf.at[k], q1_sem, k, device))

    landed(g_plane)
    g_side = sibling_gather(gram, g_sem)
    r_copies = []
    for dx, dy in plane_offsets:
        k = dy * NX + dx
        source = part.at[pl.ds(k * n_rows, n_rows)]
        r_copies.append(send(source, prod_buf.at[k], r_sem, k, plane(-dx, -dy)[0]))

    hi, lo = split(pv * -2.0)
    s = dot_nt(jnp.concatenate([hi, hi, lo], axis=1), piv_cat[...])
    inner = (noise * amp) * matern(s + twice(piv_norm) + piv_norm_row)
    g_side.wait_recv()
    full[...] = gram[...] + inner

    half = rank // 2
    tiles = half // 8
    work[...] = full[:half, :half].reshape(tiles, 8, half)
    invert(work, 0, tiles // 2)
    landed(q1)
    q_src[...] = summed(q_all[:, here], q1_buf, PLANE)
    q_line = line_reduce(q_src, q_buf, q_sem)
    invert(work, tiles // 2, tiles)
    landed(q_line)
    q_out[my_rows(core), :] = summed(q_src[core], q_buf, LINE)
    q_plane = plane_gather(q_out, q_sem)
    upper_inverse = work[...].reshape(half, half)
    lower = full[half:, :half]
    carried = dot_exact(upper_inverse, full[:half, half:])
    work[...] = (full[half:, half:] - dot_exact(lower, carried)).reshape(tiles, 8, half)
    invert(work, 0, tiles // 2)
    landed(q_plane)
    q_side = sibling_gather(q_out, q_sem)
    invert(work, tiles // 2, tiles)
    q_side.wait_recv()
    lower_inverse = work[...].reshape(half, half)

    def solved(right_side):
        top = dot_exact(upper_inverse, right_side[:half])
        below = dot_exact(lower_inverse, right_side[half:] - dot_exact(lower, top))
        return jnp.concatenate([top - dot_exact(carried, below), below], axis=0)

    projected = q_out[...]
    coefficients = solved(projected)
    coefficients = coefficients + solved(projected - dot_exact(full[...], coefficients))
    landed(r_copies)
    product = summed(part[:n_rows, :], prod_buf, PLANE)
    product_ref[...] = product
    removed = dot_exact(cross_own[...], coefficients)
    out_ref[...] = (product - removed) / noise

    for c in everything:
        c.wait_send()


def per_device(features, probes, outputscale, noise, pivots):
    n_rows, n_feat = features.shape
    n_probe = probes.shape[1]
    rank = pivots.shape[0]
    chunk = rank // NC // PLANE
    wide = PLANE * n_rows
    block = 4 * n_rows
    vmem = pltpu.VMEM
    dma = pltpu.SemaphoreType.DMA
    spread = jnp.broadcast_to(pivots[:, None], (rank, 128))
    return pl.pallas_call(
        exchange_kernel,
        out_shape=(jax.ShapeDtypeStruct((n_rows, n_probe), f32),) * 2,
        in_specs=[pl.BlockSpec(memory_space=vmem)] * 3
        + [pl.BlockSpec(memory_space=pltpu.SMEM)] * 2,
        out_specs=[pl.BlockSpec(memory_space=vmem)] * 2,
        scratch_shapes=[
            vmem((2, NY, NX, n_rows, n_feat // 2), f32),
            vmem((LINE, n_rows, n_feat + n_probe), f32),
            vmem((NC, chunk, n_feat), f32),
            vmem((LINE, chunk, n_feat), f32),
            vmem((rank, n_feat), f32),
            vmem((wide, 3 * n_feat), bf16),
            vmem((wide, 128), f32),
            vmem((1, wide), f32),
            vmem((block, 3 * n_feat), bf16),
            vmem((1, block), f32),
            vmem((block, 2 * n_probe), bf16),
            vmem((wide, n_probe), f32),
            vmem((rank, 3 * n_feat), bf16),
            vmem((rank, wide), f32),
            vmem((rank, wide), bf16),
            vmem((rank, wide), bf16),
            vmem((n_rows, rank), f32),
            vmem((NC, chunk, rank), f32),
            vmem((LINE, chunk, rank), f32),
            vmem((rank, rank), f32),
            vmem((NC, PLANE, chunk, n_probe), f32),
            vmem((PLANE, NC, chunk, n_probe), f32),
            vmem((NC, chunk, n_probe), f32),
            vmem((LINE, chunk, n_probe), f32),
            vmem((rank, n_probe), f32),
            vmem((PLANE, n_rows, n_probe), f32),
            vmem((rank // 16, 8, rank // 2), f32),
            vmem((rank, rank), f32),
            dma((2, 4 * PLANE)),
            dma((2, LINE + 1)),
            dma((2, LINE + PLANE + 1)),
            dma((2, LINE + PLANE + 1)),
            dma((2, LINE + PLANE + 1)),
            dma((2, PLANE)),
            dma((2, PLANE)),
        ],
        compiler_params=pltpu.CompilerParams(
            collective_id=0, has_side_effects=True, vmem_limit_bytes=40 * 1024 * 1024
        ),
        name="exchange",
    )(features, probes, spread, outputscale, noise)


def solution(mesh):
    in_specs = (P(("blk", "row"), None), P(("blk", "row"), None), P(), P(), P())
    out_specs = (P(("blk", "row"), None), P(("blk", "row"), None))
    return jax.shard_map(
        per_device, mesh=mesh, in_specs=in_specs, out_specs=out_specs, check_vma=False
    )
```

time: 141 us -> 77.7 us (0.55)
  other arithmetic: 53.9 us -> 0 us
  local copies, waits for them, and re-layouts: 5.04 us -> 2.06 us
  matrix products: 2.78 us -> 0 us
  Pallas kernels: 75.2 us -> 73.5 us
  between operations: 3.47 us -> 1.98 us
    another operation x9 -> x0, other arithmetic: 53.9 us -> none  [the longest x6 34.2 us: per_device(): factor = jnp.linalg.cholesky(gram)]
    another operation x9 -> x0, local copies, waits for them, and re-layouts: 4.12 us -> none
    another operation x8 -> x0, matrix products: 1.94 us -> none  [the longest x6 1.47 us: per_device(): coefficients = jax.scipy.linalg.cho_solve((factor, True), projected)]
    pallas_call x1, Pallas kernels: 75.2 us -> 73.5 us  [per_device(): pl.pallas_call(exchange_kernel, out_shape=(jax.ShapeDtypeStruct((n_rows,...]
where the time goes in v2:
time: 77.7 us; the launch traced here: 77.5 us
  Pallas kernels  73.5 us (95%)
  local copies, waits for them, and re-layouts  2.06 us (3%)
  between operations  1.98 us (3%)
    pallas_call x1, Pallas kernels, per_device(): pl.pallas_call(exchange_kernel, out_shape=(jax.ShapeDtypeStruct((n_rows,...  73.5 us
    unnamed x8, local copies, waits for them, and re-layouts  1.98 us

profile of v2, /device:TPU:1, one launch (start us, length us, event | category | flops | bytes accessed | tf_op | source)
XLA Modules:
  0.0 77.5 jit_solution(8387399472279094777)
XLA Ops:
  1.3 0.0 copy-start.2
  1.9 0.0 copy-done.2
  2.0 0.0 copy-start
  2.0 0.0 copy-start.1
  2.0 0.1 broadcast_in_dim.2.pivots_ref
  2.1 0.7 copy-done
  2.8 0.0 copy-done.1
  2.8 73.5 %exchange.1 = (f32[64,128]{1,0:T(8,128)S(1)}, f32[64,128]{1,0:T(8,128)S(1)}) custom-call(f32[64,256]{1,0:T(8,128)S(1)} %copy-done, f32[64,128]{1,0:T(8,128)S(1)} %copy-done.1, s32[256,128]{1,0:T(8,128)S(1)} %broadcast_in_dim.2.pivots_ref, f32[1]{0:T(128)S(6)} %copy.9.amp_ref, f32[1]{0:T(128)S(6)} %copy.10.noise_ref), custom_call_target="tpu_custom_call" | custom-call | tf_op jit(solution)/shard_map/exchange/pallas_call | solution.py:484
  76.3 0.6 copy.11
  76.9 0.6 copy.12
Async XLA Ops:
  1.3 0.7 copy-start.2
  2.0 0.8 %copy-start = (f32[64,256]{1,0:T(8,128)S(1)}, f32[64,256]{1,0:T(8,128)}, u32[]{:S(2)}) copy-start(f32[64,256]{1,0:T(8,128)} %feats_ref.1) | copy-start | bytes 196612
  2.0 0.8 %copy-start.1 = (f32[64,128]{1,0:T(8,128)S(1)}, f32[64,128]{1,0:T(8,128)}, u32[]{:S(2)}) copy-start(f32[64,128]{1,0:T(8,128)} %probes_ref.1) | copy-start | bytes 98308

commit v3 on v2

--- a/solution.py
+++ b/solution.py
@@ -52,7 +52,7 @@
     return jnp.dot(a, b, precision=highest, preferred_element_type=f32)
 
 
-def invert(work, first_tile, last_tile):
+def invert(work, between):
     tiles, _, half = work.shape
     sub = lax.broadcasted_iota(jnp.int32, (8, half), 0)
     lane = lax.broadcasted_iota(jnp.int32, (8, half), 1)
@@ -68,13 +68,16 @@
         r = r * (2.0 - d * r)
         return r * (2.0 - d * r)
 
-    def step(kb, carry):
-        start = kb * 8
-        index = [jnp.full((8, half), start + c, jnp.int32) for c in range(8)]
-        active = (lane >= start) & (lane < start + 8)
-        top = work[kb]
-        d = [spread_lane(top, index[c]) for c in range(8)]
-        top = jnp.where(active, jnp.where(lane - start == sub, 1.0, 0.0), top)
+    def lanes_of(block):
+        first = jnp.clip(block, 0, tiles - 1) * 8
+        return [jnp.full((8, half), first + c, jnp.int32) for c in range(8)]
+
+    def in_block(block):
+        return (lane >= block * 8) & (lane < block * 8 + 8)
+
+    def eliminated(d, top, block):
+        d = list(d)
+        top = jnp.where(in_block(block), jnp.where(lane - block * 8 == sub, 1.0, 0.0), top)
         for s in range(0, 8, 2):
             a, b, c = spread_row(d[s], s), spread_row(d[s + 1], s), spread_row(d[s + 1], s + 1)
             inverse = reciprocal(a * c - b * b)
@@ -91,26 +94,42 @@
             for c2 in range(s + 2, 8):
                 d[c2] = swept(d[c2])
             top = swept(top)
-        rows = [spread_row(top, c) for c in range(8)]
+        return top
+
+    def updated(v, mask, index, rows):
+        total = jnp.where(mask, 0.0, v)
+        for c in range(8):
+            total = total - spread_lane(v, index[c]) * rows[c]
+        return total
+
+    def step(block, carry):
+        d, top, last = carry
+        done = eliminated(d, top, block)
+        mask, index = in_block(block - 1), lanes_of(block - 1)
+        rows = [spread_row(last, c) for c in range(8)]
         for r in range(tiles):
-            v = work[r]
-            total = jnp.where(active, 0.0, v)
-            for c in range(8):
-                total = total - spread_lane(v, index[c]) * rows[c]
-            work[r] = total
-        work[kb] = top
-        return carry
-
-    lax.fori_loop(first_tile, last_tile, step, 0)
+            work[r] = updated(work[r], mask, index, rows)
+        work[jnp.maximum(block - 1, 0)] = last
+        v = work[jnp.minimum(block + 1, tiles - 1)]
+        top = updated(v, in_block(block), lanes_of(block), [spread_row(done, c) for c in range(8)])
+        index = lanes_of(block + 1)
+        return tuple(spread_lane(top, index[c]) for c in range(8)), top, done
+
+    top = work[0]
+    index = lanes_of(0)
+    carry = (tuple(spread_lane(top, index[c]) for c in range(8)), top, jnp.zeros_like(top))
+    carry = lax.fori_loop(0, tiles // 2, step, carry)
+    between()
+    lax.fori_loop(tiles // 2, tiles + 1, step, carry)
 
 
 def exchange_kernel(
     feats_ref, probes_ref, pivots_ref, amp_ref, noise_ref,
     product_ref, out_ref,
-    a_buf, b_buf, pick, p_buf, piv,
+    a_buf, b_buf, pick, p1_buf, p_src, p_buf, piv,
     r_cat, r_norm, r_norm_row, c_cat, c_norm_row, v_cat, part,
     piv_cat, ct, ct_hi, ct_lo, cross_own, g_src, g_buf, gram, q_all, q1_buf, q_src, q_buf, q_out, prod_buf, work, full,
-    a_sem, b_sem, p_sem, g_sem, q_sem, q1_sem, r_sem,
+    a_sem, b_sem, p_sem, g_sem, q_sem, p1_sem, q1_sem, r_sem,
 ):
     n_rows, n_feat = feats_ref.shape
     n_probe = probes_ref.shape[1]
@@ -165,6 +184,10 @@
     a_buf[1, 0, 0] = own[:, half_feat:]
     b_buf[0, :, :n_feat] = own
     b_buf[0, :, n_feat:] = probes_ref[...]
+    first = (blk * (NX * NZ // ZLO) + row) * n_rows
+    point = lax.broadcasted_iota(jnp.int32, (rank, n_rows), 1) + first
+    onehot = (point == pivots_ref[:, :n_rows]).astype(f32)
+    pick[...] = dot_exact(onehot, own).reshape(NC, PLANE, chunk, n_feat)
     pl.semaphore_wait(barrier, PLANE + LINE - 2)
 
     def landed(copies):
@@ -178,45 +201,27 @@
     def a_slot(h, u, v):
         return a_buf.at[(h, v, u) if h == 0 else (h, u, v)]
 
-    def a_send(h, u, v, du, dv, part_of=None):
+    def a_send(h, u, v, du, dv):
         to = ((u + du) % 4, (v + dv) % 4)
-        src, dst = a_slot(h, u, v), a_slot(h, *to)
-        if part_of is not None:
-            src, dst = src.at[part_of], dst.at[part_of]
-        index = 2 * (16 * h + 4 * to[0] + to[1]) + (part_of is lower_rows)
         device = plane(du, dv)[0] if h == 0 else plane(dv, du)[0]
-        moved[(h, *to, part_of is lower_rows)] = send(src, dst, a_sem, index, device)
+        moved[(h, *to)] = send(a_slot(h, u, v), a_slot(h, *to), a_sem, 16 * h + 4 * to[0] + to[1], device)
 
     def a_wait(*slots):
         for u, v in slots:
             for h in range(2):
-                for low in (False, True):
-                    if (h, u, v, low) in moved:
-                        moved[(h, u, v, low)].wait_recv()
-
-    def a_round(step):
-        for h in range(2):
-            if step == 0:
-                for d in (1, -1):
-                    a_send(h, 0, 0, d, 0)
-                    a_send(h, 0, 0, 0, d)
-            if step == 1:
-                a_send(h, 1, 0, 1, 0, upper_rows)
-                a_send(h, 3, 0, -1, 0, lower_rows)
-                for u in (1, 3):
-                    for d in (1, -1):
-                        a_send(h, u, 0, 0, d)
-                a_send(h, 0, 1, 0, 1, upper_rows)
-                a_send(h, 0, 3, 0, -1, lower_rows)
-            if step == 2:
-                for d in (1, -1):
-                    a_send(h, 2, 0, 0, d)
-                for u in (1, 3):
-                    a_send(h, u, 1, 0, 1, upper_rows)
-                    a_send(h, u, 3, 0, -1, lower_rows)
-            if step == 3:
-                a_send(h, 2, 1, 0, 1, upper_rows)
-                a_send(h, 2, 3, 0, -1, lower_rows)
+                moved[(h, u, v)].wait_recv()
+
+    def a_start():
+        for d in (1, -1, 2):
+            for h in range(2):
+                a_send(h, 0, 0, d, 0)
+                a_send(h, 0, 0, 0, d)
+
+    def a_forward(*steps):
+        for d in (1, -1, 2):
+            for h in range(2):
+                for u in steps:
+                    a_send(h, u, 0, 0, d)
 
     right, left = line(1, 0)[0], line(-1, 0)[0]
     sibling = line(0, 1)[0]
@@ -257,42 +262,8 @@
                 total = square if total is None else total + square
             r_norm[rows, :] = jnp.broadcast_to(jnp.sum(total, axis=1, keepdims=True), (n_rows, 128))
 
-    a_round(0)
-    ring = {1: b_send(0, 1, right), 7: b_send(0, 7, left)}
-    across = {0: b_sibling(0)}
-    prepare([(0, 0)])
-    a_wait((1, 0), (3, 0), (0, 1), (0, 3))
-    a_round(1)
-    forward(1)
-    prepare([(1, 0), (3, 0), (0, 1), (0, 3)])
-    a_wait((2, 0), (1, 1), (1, 3), (3, 1), (3, 3))
-    a_round(2)
-    forward(2)
-    a_wait((0, 2))
-    prepare([(1, 1), (1, 3), (3, 1), (3, 3), (2, 0), (0, 2)])
-    a_wait((2, 1), (2, 3))
-    a_round(3)
-    forward(3)
-    a_wait((1, 2), (3, 2), (2, 2))
-    prepare([(2, 1), (2, 3), (1, 2), (3, 2), (2, 2)])
-
     def my_rows(c):
         return pl.ds(pl.multiple_of(c * half_rank + here * chunk, chunk), chunk)
-
-    position = lax.broadcasted_iota(jnp.int32, (8, PLANE * n_rows), 1)
-    slot = position // n_rows
-    from_x = (x + NX - slot % NX) % NX
-    from_y = (y + NY - slot // NX) % NY
-    point = (((z % ZLO * NY + from_y) * NC + core) * (NX * NZ // ZLO) + z // ZLO * NX + from_x) * n_rows
-    point = point + position % n_rows
-    onehot = []
-    for c in range(NC):
-        wanted = pivots_ref[my_rows(c), :]
-        onehot.append((point == jnp.concatenate([wanted] * (PLANE * n_rows // 128), axis=1)).astype(f32))
-    onehot = jnp.concatenate(onehot, axis=0)
-    for h in range(2):
-        value = dot_exact(onehot, a_buf[h].reshape(PLANE * n_rows, half_feat))
-        pick[:, :, h * half_feat:(h + 1) * half_feat] = value.reshape(NC, chunk, half_feat)
 
     def line_reduce(src, dst, sem):
         copies = []
@@ -304,21 +275,50 @@
 
     def plane_gather(ref, sem):
         copies = []
+        mine = ref.at[my_rows(core)]
         for dx, dy in plane_offsets:
-            mine = ref.at[my_rows(core)]
-            copies.append(send(mine, mine, sem, LINE + dy * NX + dx, plane(dx, dy)[0]))
+            k = LINE + dy * NX + dx
+            (other_blk, other_row), _ = plane(dx, dy)
+            copies.append(send(mine, mine, sem, k, (other_blk, other_row)))
+            copies.append(send(mine, mine, sem, k + PLANE, (other_blk + 1 - 2 * core, other_row)))
+        copies.append(send(mine, mine, sem, LINE + PLANE, sibling))
         return copies
 
-    def sibling_gather(ref, sem):
-        mine = ref.at[pl.ds(pl.multiple_of(core * half_rank, half_rank), half_rank)]
-        return send(mine, mine, sem, LINE + PLANE, sibling)
+    def plane_scatter(src, dst, sem):
+        copies = []
+        for dx, dy in plane_offsets:
+            device, there = plane(dx, dy)
+            k = dy * NX + dx
+            copies.append(send(src.at[:, there], dst.at[k], sem, k, device))
+        return copies
 
     def summed(total, buf, count):
         for k in range(1, count):
             total = total + buf[k]
         return total
 
-    p_line = line_reduce(pick, p_buf, p_sem)
+    p_scatter = plane_scatter(pick, p1_buf, p1_sem)
+    a_start()
+    ring = {1: b_send(0, 1, right), 7: b_send(0, 7, left)}
+    across = {0: b_sibling(0)}
+    prepare([(0, 0)])
+    a_wait((1, 0), (3, 0))
+    a_forward(1, 3)
+    a_wait((2, 0))
+    a_forward(2)
+    landed(p_scatter)
+    p_src[...] = summed(pick[:, here], p1_buf, PLANE)
+    p_line = line_reduce(p_src, p_buf, p_sem)
+    forward(1)
+    a_wait((0, 1), (0, 3), (0, 2))
+    prepare([(1, 0), (3, 0), (2, 0), (0, 1), (0, 3), (0, 2)])
+    a_wait((1, 1), (1, 3), (3, 1), (3, 3), (1, 2), (3, 2), (2, 1), (2, 3), (2, 2))
+    prepare([(1, 1), (1, 3), (3, 1), (3, 3), (2, 1), (2, 3), (1, 2), (3, 2), (2, 2)])
+
+    landed(p_line)
+    piv[my_rows(core), :] = summed(p_src[core], p_buf, LINE)
+    p_plane = plane_gather(piv, p_sem)
+    forward(2)
 
     for k in range(0, r_norm.shape[0], 128):
         r_norm_row[:, k:k + 128] = as_row(r_norm[k:k + 128, :])
@@ -356,24 +356,7 @@
     across[1].wait_recv()
     columns([(0, 0), (0, 1), (1, 0), (1, 1)])
 
-    landed(p_line)
-    piv[my_rows(core), :] = summed(pick[core], p_buf, LINE)
-    p_plane = plane_gather(piv, p_sem)
-    ring[4].wait_recv()
-    ring["4b"].wait_recv()
-    across[4] = b_sibling(4)
-
-    across[2].wait_recv()
-    across[7].wait_recv()
-    columns([(7, 0), (7, 1), (2, 0), (2, 1)])
-
     landed(p_plane)
-    p_side = sibling_gather(piv, p_sem)
-    across[6].wait_recv()
-    across[3].wait_recv()
-    columns([(6, 0), (6, 1), (3, 0), (3, 1)])
-
-    p_side.wait_recv()
     pv = piv[...]
     hi, lo = split(pv)
     piv_cat[:, :n_feat] = hi
@@ -397,13 +380,26 @@
 
     s = dot_nt(r_cat[:n_rows, :], piv_cat[...])
     cross_own[...] = amp * matern(s + twice(r_norm[:n_rows, :]) + piv_norm_row)
+    forward(3)
+    across[2].wait_recv()
+    across[7].wait_recv()
+    columns([(7, 0), (7, 1), (2, 0), (2, 1)])
+    across[6].wait_recv()
+    across[3].wait_recv()
+    columns([(6, 0), (6, 1), (3, 0), (3, 1)])
+
+    landed(g_line)
+    gram[my_rows(core), :] = summed(g_src[core], g_buf, LINE)
+    g_plane = plane_gather(gram, g_sem)
+    ring[4].wait_recv()
+    ring["4b"].wait_recv()
+    across[4] = b_sibling(4)
+    hi, lo = split(pv * -2.0)
+    s = dot_nt(jnp.concatenate([hi, hi, lo], axis=1), piv_cat[...])
+    full[...] = (noise * amp) * matern(s + twice(piv_norm) + piv_norm_row)
     across[5].wait_recv()
     across[4].wait_recv()
     columns([(5, 0), (5, 1), (4, 0), (4, 1)])
-
-    landed(g_line)
-    gram[my_rows(core), :] = summed(g_src[core], g_buf, LINE)
-    g_plane = plane_gather(gram, g_sem)
 
     part[...] = part[...] * amp
     part[:n_rows, :] = part[:n_rows, :] + noise * probes_ref[...]
@@ -411,46 +407,37 @@
     both = dot_nn(ct_hi[...], jnp.concatenate([hi, lo], axis=1))
     q = both[:, :n_probe] + both[:, n_probe:] + dot_nn(ct_lo[...], hi)
     q_all[...] = q.reshape(NC, PLANE, chunk, n_probe)
-    q1 = []
-    for dx, dy in plane_offsets:
-        device, there = plane(dx, dy)
-        k = dy * NX + dx
-        q1.append(send(q_all.at[:, there], q1_buf.at[k], q1_sem, k, device))
-
+    q1 = plane_scatter(q_all, q1_buf, q1_sem)
     landed(g_plane)
-    g_side = sibling_gather(gram, g_sem)
     r_copies = []
     for dx, dy in plane_offsets:
         k = dy * NX + dx
         source = part.at[pl.ds(k * n_rows, n_rows)]
         r_copies.append(send(source, prod_buf.at[k], r_sem, k, plane(-dx, -dy)[0]))
-
-    hi, lo = split(pv * -2.0)
-    s = dot_nt(jnp.concatenate([hi, hi, lo], axis=1), piv_cat[...])
-    inner = (noise * amp) * matern(s + twice(piv_norm) + piv_norm_row)
-    g_side.wait_recv()
-    full[...] = gram[...] + inner
+    full[...] = full[...] + gram[...]
 
     half = rank // 2
     tiles = half // 8
     work[...] = full[:half, :half].reshape(tiles, 8, half)
-    invert(work, 0, tiles // 2)
-    landed(q1)
-    q_src[...] = summed(q_all[:, here], q1_buf, PLANE)
-    q_line = line_reduce(q_src, q_buf, q_sem)
-    invert(work, tiles // 2, tiles)
-    landed(q_line)
-    q_out[my_rows(core), :] = summed(q_src[core], q_buf, LINE)
-    q_plane = plane_gather(q_out, q_sem)
+    sent = {}
+
+    def reduce_projected():
+        landed(q1)
+        q_src[...] = summed(q_all[:, here], q1_buf, PLANE)
+        sent["line"] = line_reduce(q_src, q_buf, q_sem)
+
+    def gather_projected():
+        landed(sent["line"])
+        q_out[my_rows(core), :] = summed(q_src[core], q_buf, LINE)
+        sent["plane"] = plane_gather(q_out, q_sem)
+
+    invert(work, reduce_projected)
     upper_inverse = work[...].reshape(half, half)
     lower = full[half:, :half]
     carried = dot_exact(upper_inverse, full[:half, half:])
     work[...] = (full[half:, half:] - dot_exact(lower, carried)).reshape(tiles, 8, half)
-    invert(work, 0, tiles // 2)
-    landed(q_plane)
-    q_side = sibling_gather(q_out, q_sem)
-    invert(work, tiles // 2, tiles)
-    q_side.wait_recv()
+    invert(work, gather_projected)
+    landed(sent["plane"])
     lower_inverse = work[...].reshape(half, half)
 
     def solved(right_side):
@@ -490,6 +477,8 @@
         scratch_shapes=[
             vmem((2, NY, NX, n_rows, n_feat // 2), f32),
             vmem((LINE, n_rows, n_feat + n_probe), f32),
+            vmem((NC, PLANE, chunk, n_feat), f32),
+            vmem((PLANE, NC, chunk, n_feat), f32),
             vmem((NC, chunk, n_feat), f32),
             vmem((LINE, chunk, n_feat), f32),
             vmem((rank, n_feat), f32),
@@ -516,11 +505,12 @@
             vmem((PLANE, n_rows, n_probe), f32),
             vmem((rank // 16, 8, rank // 2), f32),
             vmem((rank, rank), f32),
-            dma((2, 4 * PLANE)),
+            dma((2, 2 * PLANE)),
             dma((2, LINE + 1)),
-            dma((2, LINE + PLANE + 1)),
-            dma((2, LINE + PLANE + 1)),
-            dma((2, LINE + PLANE + 1)),
+            dma((2, LINE + 2 * PLANE)),
+            dma((2, LINE + 2 * PLANE)),
+            dma((2, LINE + 2 * PLANE)),
+            dma((2, PLANE)),
             dma((2, PLANE)),
             dma((2, PLANE)),
         ],

time: 77.7 us -> 74.9 us (0.964)
  Pallas kernels: 73.5 us -> 70.7 us
    pallas_call x1, Pallas kernels: 73.5 us -> 70.7 us  [per_device(): pl.pallas_call(exchange_kernel, out_shape=(jax.ShapeDtypeStruct((n_rows,...]
where the time goes in v3:
time: 74.9 us; the launch traced here: 74.8 us
  Pallas kernels  70.7 us (94%)
  local copies, waits for them, and re-layouts  2.06 us (3%)
  between operations  1.98 us (3%)
    pallas_call x1, Pallas kernels, per_device(): pl.pallas_call(exchange_kernel, out_shape=(jax.ShapeDtypeStruct((n_rows,...  70.7 us
    unnamed x8, local copies, waits for them, and re-layouts  1.98 us

profile of v3, /device:TPU:1, one launch (start us, length us, event | category | flops | bytes accessed | tf_op | source)
XLA Modules:
  0.0 74.8 jit_solution(10558435168448227210)
XLA Ops:
  1.3 0.0 copy-start.2
  1.9 0.0 copy-done.2
  2.0 0.0 copy-start
  2.0 0.0 copy-start.1
  2.0 0.1 broadcast_in_dim.2.pivots_ref
  2.1 0.7 copy-done
  2.8 0.0 copy-done.1
  2.8 70.7 %exchange.1 = (f32[64,128]{1,0:T(8,128)S(1)}, f32[64,128]{1,0:T(8,128)S(1)}) custom-call(f32[64,256]{1,0:T(8,128)S(1)} %copy-done, f32[64,128]{1,0:T(8,128)S(1)} %copy-done.1, s32[256,128]{1,0:T(8,128)S(1)} %broadcast_in_dim.2.pivots_ref, f32[1]{0:T(128)S(6)} %copy.9.amp_ref, f32[1]{0:T(128)S(6)} %copy.10.noise_ref), custom_call_target="tpu_custom_call" | custom-call | tf_op jit(solution)/shard_map/exchange/pallas_call | solution.py:471
  73.5 0.6 copy.11
  74.1 0.6 copy.12
Async XLA Ops:
  1.3 0.7 copy-start.2
  2.0 0.8 %copy-start = (f32[64,256]{1,0:T(8,128)S(1)}, f32[64,256]{1,0:T(8,128)}, u32[]{:S(2)}) copy-start(f32[64,256]{1,0:T(8,128)} %feats_ref.1) | copy-start | bytes 196612
  2.0 0.8 %copy-start.1 = (f32[64,128]{1,0:T(8,128)S(1)}, f32[64,128]{1,0:T(8,128)}, u32[]{:S(2)}) copy-start(f32[64,128]{1,0:T(8,128)} %probes_ref.1) | copy-start | bytes 98308

commit v4 on v3

--- a/solution.py
+++ b/solution.py
@@ -52,13 +52,13 @@
     return jnp.dot(a, b, precision=highest, preferred_element_type=f32)
 
 
-def invert(work, between):
+def invert(work):
     tiles, _, half = work.shape
     sub = lax.broadcasted_iota(jnp.int32, (8, half), 0)
     lane = lax.broadcasted_iota(jnp.int32, (8, half), 1)
 
-    def spread_lane(v, index):
-        return jnp.take_along_axis(v, index, axis=1)
+    def spread_lane(v, c):
+        return jnp.take_along_axis(v, jnp.full((8, half), c, jnp.int32), axis=1)
 
     def spread_row(v, r):
         return jnp.broadcast_to(v[r:r + 1, :], v.shape)
@@ -68,59 +68,55 @@
         r = r * (2.0 - d * r)
         return r * (2.0 - d * r)
 
-    def lanes_of(block):
-        first = jnp.clip(block, 0, tiles - 1) * 8
-        return [jnp.full((8, half), first + c, jnp.int32) for c in range(8)]
-
     def in_block(block):
         return (lane >= block * 8) & (lane < block * 8 + 8)
 
-    def eliminated(d, top, block):
-        d = list(d)
+    def eliminated(top, block):
+        d = [spread_lane(top, 8 * block + c) for c in range(8)]
         top = jnp.where(in_block(block), jnp.where(lane - block * 8 == sub, 1.0, 0.0), top)
         for s in range(0, 8, 2):
             a, b, c = spread_row(d[s], s), spread_row(d[s + 1], s), spread_row(d[s + 1], s + 1)
             inverse = reciprocal(a * c - b * b)
-            a, b, c = a * inverse, b * inverse, c * inverse
             first, second = d[s], d[s + 1]
 
             def swept(v):
                 r0, r1 = spread_row(v, s), spread_row(v, s + 1)
-                p0 = c * r0 - b * r1
-                p1 = a * r1 - b * r0
-                rest = v - first * p0 - second * p1
-                return jnp.where(sub == s, p0, jnp.where(sub == s + 1, p1, rest))
+                n0 = c * r0 - b * r1
+                n1 = a * r1 - b * r0
+                taken = jnp.where(sub == s, n0, jnp.where(sub == s + 1, n1, -(first * n0 + second * n1)))
+                kept = jnp.where((sub == s) | (sub == s + 1), 0.0, v)
+                return kept + taken * inverse
 
             for c2 in range(s + 2, 8):
                 d[c2] = swept(d[c2])
             top = swept(top)
         return top
 
-    def updated(v, mask, index, rows):
-        total = jnp.where(mask, 0.0, v)
+    def updated(v, block, rows):
+        total = jnp.where(in_block(block), 0.0, v)
         for c in range(8):
-            total = total - spread_lane(v, index[c]) * rows[c]
+            total = total - spread_lane(v, 8 * block + c) * rows[c]
         return total
 
-    def step(block, carry):
-        d, top, last = carry
-        done = eliminated(d, top, block)
-        mask, index = in_block(block - 1), lanes_of(block - 1)
-        rows = [spread_row(last, c) for c in range(8)]
-        for r in range(tiles):
-            work[r] = updated(work[r], mask, index, rows)
-        work[jnp.maximum(block - 1, 0)] = last
-        v = work[jnp.minimum(block + 1, tiles - 1)]
-        top = updated(v, in_block(block), lanes_of(block), [spread_row(done, c) for c in range(8)])
-        index = lanes_of(block + 1)
-        return tuple(spread_lane(top, index[c]) for c in range(8)), top, done
-
-    top = work[0]
-    index = lanes_of(0)
-    carry = (tuple(spread_lane(top, index[c]) for c in range(8)), top, jnp.zeros_like(top))
-    carry = lax.fori_loop(0, tiles // 2, step, carry)
-    between()
-    lax.fori_loop(tiles // 2, tiles + 1, step, carry)
+    panel = tiles // 4
+    for p in range(0, tiles, panel):
+        block_rows = [work[p + i] for i in range(panel)]
+        for i in range(panel):
+            done = eliminated(block_rows[i], p + i)
+            rows = [spread_row(done, c) for c in range(8)]
+            for other in range(panel):
+                if other != i:
+                    block_rows[other] = updated(block_rows[other], p + i, rows)
+            block_rows[i] = done
+        reduced = jnp.concatenate(block_rows, axis=0)
+        whole = work[...].reshape(half, half)
+        first, last = 8 * p, 8 * (p + panel)
+        column = lax.broadcasted_iota(jnp.int32, (half, half), 1)
+        rest = jnp.where((column >= first) & (column < last), 0.0, whole)
+        rest = rest - dot_exact(whole[:, first:last], reduced)
+        work[...] = rest.reshape(tiles, 8, half)
+        for i in range(panel):
+            work[p + i] = block_rows[i]
 
 
 def exchange_kernel(
@@ -298,27 +294,27 @@
         return total
 
     p_scatter = plane_scatter(pick, p1_buf, p1_sem)
-    a_start()
     ring = {1: b_send(0, 1, right), 7: b_send(0, 7, left)}
     across = {0: b_sibling(0)}
+    a_start()
     prepare([(0, 0)])
     a_wait((1, 0), (3, 0))
     a_forward(1, 3)
+    forward(1)
     a_wait((2, 0))
     a_forward(2)
     landed(p_scatter)
     p_src[...] = summed(pick[:, here], p1_buf, PLANE)
     p_line = line_reduce(p_src, p_buf, p_sem)
-    forward(1)
     a_wait((0, 1), (0, 3), (0, 2))
     prepare([(1, 0), (3, 0), (2, 0), (0, 1), (0, 3), (0, 2)])
-    a_wait((1, 1), (1, 3), (3, 1), (3, 3), (1, 2), (3, 2), (2, 1), (2, 3), (2, 2))
-    prepare([(1, 1), (1, 3), (3, 1), (3, 3), (2, 1), (2, 3), (1, 2), (3, 2), (2, 2)])
-
+    forward(2)
     landed(p_line)
     piv[my_rows(core), :] = summed(p_src[core], p_buf, LINE)
     p_plane = plane_gather(piv, p_sem)
-    forward(2)
+    a_wait((1, 1), (1, 3), (3, 1), (3, 3), (1, 2), (3, 2), (2, 1), (2, 3), (2, 2))
+    prepare([(1, 1), (1, 3), (3, 1), (3, 3), (2, 1), (2, 3), (1, 2), (3, 2), (2, 2)])
+    forward(3)
 
     for k in range(0, r_norm.shape[0], 128):
         r_norm_row[:, k:k + 128] = as_row(r_norm[k:k + 128, :])
@@ -350,12 +346,15 @@
             part[rows, :] = part[rows, :] + (both[:, :n_probe] + both[:, n_probe:] + last)
             return carry
 
-        lax.fori_loop(0, part.shape[0] // tile, body, 0)
+        lax.fori_loop(0, part.shape[0] // tile, body, 0, unroll=2)
 
     across[0].wait_recv()
     across[1].wait_recv()
     columns([(0, 0), (0, 1), (1, 0), (1, 1)])
 
+    across[2].wait_recv()
+    across[7].wait_recv()
+    columns([(7, 0), (7, 1), (2, 0), (2, 1)])
     landed(p_plane)
     pv = piv[...]
     hi, lo = split(pv)
@@ -378,25 +377,12 @@
     g_src[...] = g.reshape(NC, chunk, rank)
     g_line = line_reduce(g_src, g_buf, g_sem)
 
-    s = dot_nt(r_cat[:n_rows, :], piv_cat[...])
-    cross_own[...] = amp * matern(s + twice(r_norm[:n_rows, :]) + piv_norm_row)
-    forward(3)
-    across[2].wait_recv()
-    across[7].wait_recv()
-    columns([(7, 0), (7, 1), (2, 0), (2, 1)])
+    ring[4].wait_recv()
+    ring["4b"].wait_recv()
+    across[4] = b_sibling(4)
     across[6].wait_recv()
     across[3].wait_recv()
     columns([(6, 0), (6, 1), (3, 0), (3, 1)])
-
-    landed(g_line)
-    gram[my_rows(core), :] = summed(g_src[core], g_buf, LINE)
-    g_plane = plane_gather(gram, g_sem)
-    ring[4].wait_recv()
-    ring["4b"].wait_recv()
-    across[4] = b_sibling(4)
-    hi, lo = split(pv * -2.0)
-    s = dot_nt(jnp.concatenate([hi, hi, lo], axis=1), piv_cat[...])
-    full[...] = (noise * amp) * matern(s + twice(piv_norm) + piv_norm_row)
     across[5].wait_recv()
     across[4].wait_recv()
     columns([(5, 0), (5, 1), (4, 0), (4, 1)])
@@ -408,6 +394,19 @@
     q = both[:, :n_probe] + both[:, n_probe:] + dot_nn(ct_lo[...], hi)
     q_all[...] = q.reshape(NC, PLANE, chunk, n_probe)
     q1 = plane_scatter(q_all, q1_buf, q1_sem)
+
+    landed(g_line)
+    gram[my_rows(core), :] = summed(g_src[core], g_buf, LINE)
+    g_plane = plane_gather(gram, g_sem)
+    s = dot_nt(r_cat[:n_rows, :], piv_cat[...])
+    cross_own[...] = amp * matern(s + twice(r_norm[:n_rows, :]) + piv_norm_row)
+    hi, lo = split(pv * -2.0)
+    s = dot_nt(jnp.concatenate([hi, hi, lo], axis=1), piv_cat[...])
+    full[...] = (noise * amp) * matern(s + twice(piv_norm) + piv_norm_row)
+
+    landed(q1)
+    q_src[...] = summed(q_all[:, here], q1_buf, PLANE)
+    q_line = line_reduce(q_src, q_buf, q_sem)
     landed(g_plane)
     r_copies = []
     for dx, dy in plane_offsets:
@@ -419,25 +418,16 @@
     half = rank // 2
     tiles = half // 8
     work[...] = full[:half, :half].reshape(tiles, 8, half)
-    sent = {}
-
-    def reduce_projected():
-        landed(q1)
-        q_src[...] = summed(q_all[:, here], q1_buf, PLANE)
-        sent["line"] = line_reduce(q_src, q_buf, q_sem)
-
-    def gather_projected():
-        landed(sent["line"])
-        q_out[my_rows(core), :] = summed(q_src[core], q_buf, LINE)
-        sent["plane"] = plane_gather(q_out, q_sem)
-
-    invert(work, reduce_projected)
+    invert(work)
+    landed(q_line)
+    q_out[my_rows(core), :] = summed(q_src[core], q_buf, LINE)
+    q_plane = plane_gather(q_out, q_sem)
     upper_inverse = work[...].reshape(half, half)
     lower = full[half:, :half]
     carried = dot_exact(upper_inverse, full[:half, half:])
     work[...] = (full[half:, half:] - dot_exact(lower, carried)).reshape(tiles, 8, half)
-    invert(work, gather_projected)
-    landed(sent["plane"])
+    invert(work)
+    landed(q_plane)
     lower_inverse = work[...].reshape(half, half)
 
     def solved(right_side):

time: 74.9 us -> 69.8 us (0.932)
  Pallas kernels: 70.7 us -> 65.6 us
    pallas_call x1, Pallas kernels: 70.7 us -> 65.6 us  [per_device(): pl.pallas_call(exchange_kernel, out_shape=(jax.ShapeDtypeStruct((n_rows,...]
where the time goes in v4:
time: 69.8 us; the launch traced here: 69.7 us
  Pallas kernels  65.6 us (94%)
  local copies, waits for them, and re-layouts  2.06 us (3%)
  between operations  1.98 us (3%)
    pallas_call x1, Pallas kernels, per_device(): pl.pallas_call(exchange_kernel, out_shape=(jax.ShapeDtypeStruct((n_rows,...  65.6 us
    unnamed x8, local copies, waits for them, and re-layouts  1.98 us

profile of v4, /device:TPU:1, one launch (start us, length us, event | category | flops | bytes accessed | tf_op | source)
XLA Modules:
  0.0 69.7 jit_solution(1399118536420149272)
XLA Ops:
  1.3 0.0 copy-start.2
  1.9 0.0 copy-done.2
  2.0 0.0 copy-start
  2.0 0.0 copy-start.1
  2.0 0.1 broadcast_in_dim.2.pivots_ref
  2.1 0.7 %copy-done = f32[64,256]{1,0:T(8,128)S(1)} copy-done((f32[64,256]{1,0:T(8,128)S(1)}, f32[64,256]{1,0:T(8,128)}, u32[]{:S(2)}) %copy-start) | copy-done | bytes 65560
  2.8 0.0 copy-done.1
  2.8 65.6 %exchange.1 = (f32[64,128]{1,0:T(8,128)S(1)}, f32[64,128]{1,0:T(8,128)S(1)}) custom-call(f32[64,256]{1,0:T(8,128)S(1)} %copy-done, f32[64,128]{1,0:T(8,128)S(1)} %copy-done.1, s32[256,128]{1,0:T(8,128)S(1)} %broadcast_in_dim.2.pivots_ref, f32[1]{0:T(128)S(6)} %copy.9.amp_ref, f32[1]{0:T(128)S(6)} %copy.10.noise_ref), custom_call_target="tpu_custom_call" | custom-call | tf_op jit(solution)/shard_map/exchange/pallas_call | solution.py:461
  68.4 0.6 copy.11
  69.0 0.6 copy.12
Async XLA Ops:
  1.3 0.7 copy-start.2
  2.0 0.8 %copy-start = (f32[64,256]{1,0:T(8,128)S(1)}, f32[64,256]{1,0:T(8,128)}, u32[]{:S(2)}) copy-start(f32[64,256]{1,0:T(8,128)} %feats_ref.1) | copy-start | bytes 196612
  2.0 0.8 %copy-start.1 = (f32[64,128]{1,0:T(8,128)S(1)}, f32[64,128]{1,0:T(8,128)}, u32[]{:S(2)}) copy-start(f32[64,128]{1,0:T(8,128)} %probes_ref.1) | copy-start | bytes 98308

commit v5 on v4

--- a/solution.py
+++ b/solution.py
@@ -125,7 +125,7 @@
     a_buf, b_buf, pick, p1_buf, p_src, p_buf, piv,
     r_cat, r_norm, r_norm_row, c_cat, c_norm_row, v_cat, part,
     piv_cat, ct, ct_hi, ct_lo, cross_own, g_src, g_buf, gram, q_all, q1_buf, q_src, q_buf, q_out, prod_buf, work, full,
-    a_sem, b_sem, p_sem, g_sem, q_sem, p1_sem, q1_sem, r_sem,
+    a_sem, b_sem, stage_sem,
 ):
     n_rows, n_feat = feats_ref.shape
     n_probe = probes_ref.shape[1]
@@ -157,15 +157,12 @@
         key=lambda o: -min(o[0], NZ - o[0]),
     )
 
-    everything = []
-
     def send(src, dst, sem, k, device):
         copy = pltpu.make_async_remote_copy(
             src_ref=src, dst_ref=dst, send_sem=sem.at[0, k], recv_sem=sem.at[1, k],
             device_id=device, device_id_type=MESH,
         )
         copy.start()
-        everything.append(copy)
         return copy
 
     barrier = pltpu.get_barrier_semaphore()
@@ -185,10 +182,6 @@
     onehot = (point == pivots_ref[:, :n_rows]).astype(f32)
     pick[...] = dot_exact(onehot, own).reshape(NC, PLANE, chunk, n_feat)
     pl.semaphore_wait(barrier, PLANE + LINE - 2)
-
-    def landed(copies):
-        for c in copies:
-            c.wait_recv()
 
     upper_rows, lower_rows = pl.ds(0, n_rows // 2), pl.ds(n_rows // 2, n_rows // 2)
 
@@ -261,39 +254,47 @@
     def my_rows(c):
         return pl.ds(pl.multiple_of(c * half_rank + here * chunk, chunk), chunk)
 
-    def line_reduce(src, dst, sem):
+    def stage(copies, number, whole):
+        for src, dst, device in copies:
+            pltpu.make_async_remote_copy(
+                src_ref=src, dst_ref=dst, send_sem=stage_sem.at[0, number], recv_sem=stage_sem.at[1, number],
+                device_id=device, device_id_type=MESH,
+            ).start()
+        return pltpu.make_async_remote_copy(
+            src_ref=whole, dst_ref=whole, send_sem=stage_sem.at[0, number], recv_sem=stage_sem.at[1, number],
+            device_id=sibling, device_id_type=MESH,
+        )
+
+    def line_reduce(src, dst, number):
         copies = []
         for dz, dc in line_offsets:
             device, cc = line(dz, dc)
-            k = dz * NC + dc
-            copies.append(send(src.at[cc], dst.at[k], sem, k, device))
-        return copies
-
-    def plane_gather(ref, sem):
+            copies.append((src.at[cc], dst.at[dz * NC + dc], device))
+        return stage(copies, number, dst.at[pl.ds(1, LINE - 1)])
+
+    def plane_gather(ref, number):
         copies = []
         mine = ref.at[my_rows(core)]
         for dx, dy in plane_offsets:
-            k = LINE + dy * NX + dx
             (other_blk, other_row), _ = plane(dx, dy)
-            copies.append(send(mine, mine, sem, k, (other_blk, other_row)))
-            copies.append(send(mine, mine, sem, k + PLANE, (other_blk + 1 - 2 * core, other_row)))
-        copies.append(send(mine, mine, sem, LINE + PLANE, sibling))
-        return copies
-
-    def plane_scatter(src, dst, sem):
+            copies.append((mine, mine, (other_blk, other_row)))
+            copies.append((mine, mine, (other_blk + 1 - 2 * core, other_row)))
+        copies.append((mine, mine, sibling))
+        return stage(copies, number, ref.at[pl.ds(0, len(copies) * chunk)])
+
+    def plane_scatter(src, dst, number):
         copies = []
         for dx, dy in plane_offsets:
             device, there = plane(dx, dy)
-            k = dy * NX + dx
-            copies.append(send(src.at[:, there], dst.at[k], sem, k, device))
-        return copies
+            copies.append((src.at[:, there], dst.at[dy * NX + dx], device))
+        return stage(copies, number, dst.at[pl.ds(1, PLANE - 1)])
 
     def summed(total, buf, count):
         for k in range(1, count):
             total = total + buf[k]
         return total
 
-    p_scatter = plane_scatter(pick, p1_buf, p1_sem)
+    p_scatter = plane_scatter(pick, p1_buf, 0)
     ring = {1: b_send(0, 1, right), 7: b_send(0, 7, left)}
     across = {0: b_sibling(0)}
     a_start()
@@ -303,15 +304,15 @@
     forward(1)
     a_wait((2, 0))
     a_forward(2)
-    landed(p_scatter)
+    p_scatter.wait_recv()
     p_src[...] = summed(pick[:, here], p1_buf, PLANE)
-    p_line = line_reduce(p_src, p_buf, p_sem)
+    p_line = line_reduce(p_src, p_buf, 1)
     a_wait((0, 1), (0, 3), (0, 2))
     prepare([(1, 0), (3, 0), (2, 0), (0, 1), (0, 3), (0, 2)])
     forward(2)
-    landed(p_line)
+    p_line.wait_recv()
     piv[my_rows(core), :] = summed(p_src[core], p_buf, LINE)
-    p_plane = plane_gather(piv, p_sem)
+    p_plane = plane_gather(piv, 2)
     a_wait((1, 1), (1, 3), (3, 1), (3, 3), (1, 2), (3, 2), (2, 1), (2, 3), (2, 2))
     prepare([(1, 1), (1, 3), (3, 1), (3, 3), (2, 1), (2, 3), (1, 2), (3, 2), (2, 2)])
     forward(3)
@@ -355,7 +356,11 @@
     across[2].wait_recv()
     across[7].wait_recv()
     columns([(7, 0), (7, 1), (2, 0), (2, 1)])
-    landed(p_plane)
+    for c in list(moved.values()) + [ring[k] for k in (1, 2, 3, 5, 6, 7)]:
+        c.wait_send()
+    p_scatter.wait_send()
+    p_line.wait_send()
+    p_plane.wait_recv()
     pv = piv[...]
     hi, lo = split(pv)
     piv_cat[:, :n_feat] = hi
@@ -375,7 +380,7 @@
     both = dot_nt(jnp.concatenate([hi, lo], axis=0), ct_hi[...])
     g = both[:NC * chunk] + both[NC * chunk:] + dot_nt(hi, ct_lo[...])
     g_src[...] = g.reshape(NC, chunk, rank)
-    g_line = line_reduce(g_src, g_buf, g_sem)
+    g_line = line_reduce(g_src, g_buf, 3)
 
     ring[4].wait_recv()
     ring["4b"].wait_recv()
@@ -393,41 +398,50 @@
     both = dot_nn(ct_hi[...], jnp.concatenate([hi, lo], axis=1))
     q = both[:, :n_probe] + both[:, n_probe:] + dot_nn(ct_lo[...], hi)
     q_all[...] = q.reshape(NC, PLANE, chunk, n_probe)
-    q1 = plane_scatter(q_all, q1_buf, q1_sem)
-
-    landed(g_line)
+    q1 = plane_scatter(q_all, q1_buf, 5)
+
+    for step in (4, "4b"):
+        ring[step].wait_send()
+    for copy in across.values():
+        copy.wait_send()
+    p_plane.wait_send()
+    g_line.wait_recv()
     gram[my_rows(core), :] = summed(g_src[core], g_buf, LINE)
-    g_plane = plane_gather(gram, g_sem)
+    g_plane = plane_gather(gram, 4)
     s = dot_nt(r_cat[:n_rows, :], piv_cat[...])
     cross_own[...] = amp * matern(s + twice(r_norm[:n_rows, :]) + piv_norm_row)
     hi, lo = split(pv * -2.0)
     s = dot_nt(jnp.concatenate([hi, hi, lo], axis=1), piv_cat[...])
     full[...] = (noise * amp) * matern(s + twice(piv_norm) + piv_norm_row)
 
-    landed(q1)
+    g_line.wait_send()
+    q1.wait_recv()
     q_src[...] = summed(q_all[:, here], q1_buf, PLANE)
-    q_line = line_reduce(q_src, q_buf, q_sem)
-    landed(g_plane)
+    q_line = line_reduce(q_src, q_buf, 6)
+    g_plane.wait_recv()
     r_copies = []
     for dx, dy in plane_offsets:
         k = dy * NX + dx
         source = part.at[pl.ds(k * n_rows, n_rows)]
-        r_copies.append(send(source, prod_buf.at[k], r_sem, k, plane(-dx, -dy)[0]))
+        r_copies.append((source, prod_buf.at[k], plane(-dx, -dy)[0]))
+    r_stage = stage(r_copies, 8, prod_buf.at[pl.ds(1, PLANE - 1)])
     full[...] = full[...] + gram[...]
 
     half = rank // 2
     tiles = half // 8
     work[...] = full[:half, :half].reshape(tiles, 8, half)
     invert(work)
-    landed(q_line)
+    q_line.wait_recv()
     q_out[my_rows(core), :] = summed(q_src[core], q_buf, LINE)
-    q_plane = plane_gather(q_out, q_sem)
+    q_plane = plane_gather(q_out, 7)
     upper_inverse = work[...].reshape(half, half)
     lower = full[half:, :half]
     carried = dot_exact(upper_inverse, full[:half, half:])
     work[...] = (full[half:, half:] - dot_exact(lower, carried)).reshape(tiles, 8, half)
     invert(work)
-    landed(q_plane)
+    for later in (g_plane, q1, q_line, r_stage):
+        later.wait_send()
+    q_plane.wait_recv()
     lower_inverse = work[...].reshape(half, half)
 
     def solved(right_side):
@@ -438,14 +452,13 @@
     projected = q_out[...]
     coefficients = solved(projected)
     coefficients = coefficients + solved(projected - dot_exact(full[...], coefficients))
-    landed(r_copies)
+    r_stage.wait_recv()
     product = summed(part[:n_rows, :], prod_buf, PLANE)
     product_ref[...] = product
     removed = dot_exact(cross_own[...], coefficients)
     out_ref[...] = (product - removed) / noise
 
-    for c in everything:
-        c.wait_send()
+    q_plane.wait_send()
 
 
 def per_device(features, probes, outputscale, noise, pivots):
@@ -497,12 +510,7 @@
             vmem((rank, rank), f32),
             dma((2, 2 * PLANE)),
             dma((2, LINE + 1)),
-            dma((2, LINE + 2 * PLANE)),
-            dma((2, LINE + 2 * PLANE)),
-            dma((2, LINE + 2 * PLANE)),
-            dma((2, PLANE)),
-            dma((2, PLANE)),
-            dma((2, PLANE)),
+            dma((2, 9)),
         ],
         compiler_params=pltpu.CompilerParams(
             collective_id=0, has_side_effects=True, vmem_limit_bytes=40 * 1024 * 1024

time: 69.8 us -> 65.9 us (0.944)
  Pallas kernels: 65.6 us -> 61.7 us
    pallas_call x1, Pallas kernels: 65.6 us -> 61.7 us  [per_device(): pl.pallas_call(exchange_kernel, out_shape=(jax.ShapeDtypeStruct((n_rows,...]
where the time goes in v5:
time: 65.9 us; the launch traced here: 65.7 us
  Pallas kernels  61.7 us (94%)
  local copies, waits for them, and re-layouts  2.06 us (3%)
  between operations  1.98 us (3%)
    pallas_call x1, Pallas kernels, per_device(): pl.pallas_call(exchange_kernel, out_shape=(jax.ShapeDtypeStruct((n_rows,...  61.7 us
    unnamed x8, local copies, waits for them, and re-layouts  1.98 us

profile of v5, /device:TPU:1, one launch (start us, length us, event | category | flops | bytes accessed | tf_op | source)
XLA Modules:
  0.0 65.7 jit_solution(16795957773184770376)
XLA Ops:
  1.3 0.0 copy-start.2
  1.9 0.0 copy-done.2
  2.0 0.0 copy-start
  2.0 0.0 copy-start.1
  2.0 0.1 broadcast_in_dim.2.pivots_ref
  2.1 0.7 %copy-done = f32[64,256]{1,0:T(8,128)S(1)} copy-done((f32[64,256]{1,0:T(8,128)S(1)}, f32[64,256]{1,0:T(8,128)}, u32[]{:S(2)}) %copy-start) | copy-done | bytes 65560
  2.8 0.0 copy-done.1
  2.8 61.7 %exchange.1 = (f32[64,128]{1,0:T(8,128)S(1)}, f32[64,128]{1,0:T(8,128)S(1)}) custom-call(f32[64,256]{1,0:T(8,128)S(1)} %copy-done, f32[64,128]{1,0:T(8,128)S(1)} %copy-done.1, s32[256,128]{1,0:T(8,128)S(1)} %broadcast_in_dim.2.pivots_ref, f32[1]{0:T(128)S(6)} %copy.9.amp_ref, f32[1]{0:T(128)S(6)} %copy.10.noise_ref), custom_call_target="tpu_custom_call" | custom-call | tf_op jit(solution)/shard_map/exchange/pallas_call | solution.py:474
  64.5 0.6 copy.11
  65.1 0.6 copy.12
Async XLA Ops:
  1.3 0.7 %copy-start.2 = (s32[256]{0:T(256)S(1)}, s32[256]{0:T(256)}, u32[]{:S(2)}) copy-start(s32[256]{0:T(256)} %param.9) | copy-start | bytes 3076
  2.0 0.8 %copy-start = (f32[64,256]{1,0:T(8,128)S(1)}, f32[64,256]{1,0:T(8,128)}, u32[]{:S(2)}) copy-start(f32[64,256]{1,0:T(8,128)} %feats_ref.1) | copy-start | bytes 196612
  2.0 0.8 %copy-start.1 = (f32[64,128]{1,0:T(8,128)S(1)}, f32[64,128]{1,0:T(8,128)}, u32[]{:S(2)}) copy-start(f32[64,128]{1,0:T(8,128)} %probes_ref.1) | copy-start | bytes 98308

commit v6 on v5

--- a/solution.py
+++ b/solution.py
@@ -121,7 +121,7 @@
 
 def exchange_kernel(
     feats_ref, probes_ref, pivots_ref, amp_ref, noise_ref,
-    product_ref, out_ref,
+    product_ref, own_ref, out_ref,
     a_buf, b_buf, pick, p1_buf, p_src, p_buf, piv,
     r_cat, r_norm, r_norm_row, c_cat, c_norm_row, v_cat, part,
     piv_cat, ct, ct_hi, ct_lo, cross_own, g_src, g_buf, gram, q_all, q1_buf, q_src, q_buf, q_out, prod_buf, work, full,
@@ -347,7 +347,7 @@
             part[rows, :] = part[rows, :] + (both[:, :n_probe] + both[:, n_probe:] + last)
             return carry
 
-        lax.fori_loop(0, part.shape[0] // tile, body, 0, unroll=2)
+        lax.fori_loop(0, part.shape[0] // tile, body, 0, unroll=4)
 
     across[0].wait_recv()
     across[1].wait_recv()
@@ -453,10 +453,9 @@
     coefficients = solved(projected)
     coefficients = coefficients + solved(projected - dot_exact(full[...], coefficients))
     r_stage.wait_recv()
-    product = summed(part[:n_rows, :], prod_buf, PLANE)
-    product_ref[...] = product
-    removed = dot_exact(cross_own[...], coefficients)
-    out_ref[...] = (product - removed) / noise
+    product_ref[...] = summed(prod_buf[1], prod_buf.at[pl.ds(1, PLANE - 1)], PLANE - 1)
+    own_ref[...] = part[:n_rows, :]
+    out_ref[...] = dot_exact(cross_own[...], coefficients)
 
     q_plane.wait_send()
 
@@ -471,12 +470,12 @@
     vmem = pltpu.VMEM
     dma = pltpu.SemaphoreType.DMA
     spread = jnp.broadcast_to(pivots[:, None], (rank, 128))
-    return pl.pallas_call(
+    others, own, removed = pl.pallas_call(
         exchange_kernel,
-        out_shape=(jax.ShapeDtypeStruct((n_rows, n_probe), f32),) * 2,
+        out_shape=(jax.ShapeDtypeStruct((n_rows, n_probe), f32),) * 3,
         in_specs=[pl.BlockSpec(memory_space=vmem)] * 3
         + [pl.BlockSpec(memory_space=pltpu.SMEM)] * 2,
-        out_specs=[pl.BlockSpec(memory_space=vmem)] * 2,
+        out_specs=[pl.BlockSpec(memory_space=vmem)] * 3,
         scratch_shapes=[
             vmem((2, NY, NX, n_rows, n_feat // 2), f32),
             vmem((LINE, n_rows, n_feat + n_probe), f32),
@@ -517,6 +516,8 @@
         ),
         name="exchange",
     )(features, probes, spread, outputscale, noise)
+    product = own + others
+    return product, (product - removed) / noise[0]
 
 
 def solution(mesh):

time: 65.9 us -> 64.1 us (0.973)
  local copies, waits for them, and re-layouts: 2.06 us -> 0.83 us
  Pallas kernels: 61.7 us -> 60.5 us
    unnamed x8 -> x6, local copies, waits for them, and re-layouts: 1.98 us -> 0.74 us
    pallas_call x1, Pallas kernels: 61.7 us -> 60.5 us  [per_device(): pl.pallas_call(exchange_kernel, out_shape=(jax.ShapeDtypeStruct((n_rows,...]
where the time goes in v6:
time: 64.1 us; the launch traced here: 64 us
  Pallas kernels  60.5 us (94%)
  between operations  1.98 us (3%)
  local copies, waits for them, and re-layouts  0.83 us (1%)
    pallas_call x1, Pallas kernels, per_device(): pl.pallas_call(exchange_kernel, out_shape=(jax.ShapeDtypeStruct((n_rows,...  60.5 us

profile of v6, /device:TPU:1, one launch (start us, length us, event | category | flops | bytes accessed | tf_op | source)
XLA Modules:
  0.0 64.0 jit_solution(1954199643277712643)
XLA Ops:
  1.3 0.0 copy-start.2
  1.9 0.0 copy-done.2
  2.0 0.0 copy-start
  2.0 0.0 copy-start.1
  2.0 0.1 broadcast_in_dim.2.pivots_ref
  2.1 0.7 %copy-done = f32[64,256]{1,0:T(8,128)S(1)} copy-done((f32[64,256]{1,0:T(8,128)S(1)}, f32[64,256]{1,0:T(8,128)}, u32[]{:S(2)}) %copy-start) | copy-done | bytes 65560
  2.8 0.0 copy-done.1
  2.8 60.5 %exchange.1 = (f32[64,128]{1,0:T(8,128)S(1)}, f32[64,128]{1,0:T(8,128)S(1)}, f32[64,128]{1,0:T(8,128)S(1)}) custom-call(f32[64,256]{1,0:T(8,128)S(1)} %copy-done, f32[64,128]{1,0:T(8,128)S(1)} %copy-done.1, s32[256,128]{1,0:T(8,128)S(1)} %broadcast_in_dim.2.pivots_ref, f32[1]{0:T(128)S(6)} %copy.7.amp_ref, f32[1]{0:T(128)} %copy.8.noise_ref), custom_call_target="tpu_custom_call" | custom-call | tf_op jit(solution)/shard_map/exchange/pallas_call | solution.py:473
  63.3 0.6 subtract_divide_fusion
Async XLA Ops:
  1.3 0.7 %copy-start.2 = (s32[256]{0:T(256)S(1)}, s32[256]{0:T(256)}, u32[]{:S(2)}) copy-start(s32[256]{0:T(256)} %param.9) | copy-start | bytes 3076
  2.0 0.8 %copy-start = (f32[64,256]{1,0:T(8,128)S(1)}, f32[64,256]{1,0:T(8,128)}, u32[]{:S(2)}) copy-start(f32[64,256]{1,0:T(8,128)} %feats_ref.1) | copy-start | bytes 196612
  2.0 0.8 %copy-start.1 = (f32[64,128]{1,0:T(8,128)S(1)}, f32[64,128]{1,0:T(8,128)}, u32[]{:S(2)}) copy-start(f32[64,128]{1,0:T(8,128)} %probes_ref.1) | copy-start | bytes 98308

commit v7 on v6

--- a/solution.py
+++ b/solution.py
@@ -302,11 +302,11 @@
     a_wait((1, 0), (3, 0))
     a_forward(1, 3)
     forward(1)
-    a_wait((2, 0))
-    a_forward(2)
     p_scatter.wait_recv()
     p_src[...] = summed(pick[:, here], p1_buf, PLANE)
     p_line = line_reduce(p_src, p_buf, 1)
+    a_wait((2, 0))
+    a_forward(2)
     a_wait((0, 1), (0, 3), (0, 2))
     prepare([(1, 0), (3, 0), (2, 0), (0, 1), (0, 3), (0, 2)])
     forward(2)

time: 64.1 us -> 64 us (level)
  no operation moved by 1% of the time
where the time goes in v7:
time: 64 us; the launch traced here: 63.9 us
  Pallas kernels  60.4 us (94%)
  between operations  1.98 us (3%)
  local copies, waits for them, and re-layouts  0.83 us (1%)
    pallas_call x1, Pallas kernels, per_device(): pl.pallas_call(exchange_kernel, out_shape=(jax.ShapeDtypeStruct((n_rows,...  60.4 us

profile of v7, /device:TPU:1, one launch (start us, length us, event | category | flops | bytes accessed | tf_op | source)
XLA Modules:
  0.0 63.9 jit_solution(1435828493262888295)
XLA Ops:
  1.3 0.0 copy-start.2
  1.9 0.0 copy-done.2
  2.0 0.0 copy-start
  2.0 0.0 copy-start.1
  2.0 0.1 broadcast_in_dim.2.pivots_ref
  2.1 0.7 %copy-done = f32[64,256]{1,0:T(8,128)S(1)} copy-done((f32[64,256]{1,0:T(8,128)S(1)}, f32[64,256]{1,0:T(8,128)}, u32[]{:S(2)}) %copy-start) | copy-done | bytes 65560
  2.8 0.0 copy-done.1
  2.8 60.4 %exchange.1 = (f32[64,128]{1,0:T(8,128)S(1)}, f32[64,128]{1,0:T(8,128)S(1)}, f32[64,128]{1,0:T(8,128)S(1)}) custom-call(f32[64,256]{1,0:T(8,128)S(1)} %copy-done, f32[64,128]{1,0:T(8,128)S(1)} %copy-done.1, s32[256,128]{1,0:T(8,128)S(1)} %broadcast_in_dim.2.pivots_ref, f32[1]{0:T(128)S(6)} %copy.7.amp_ref, f32[1]{0:T(128)} %copy.8.noise_ref), custom_call_target="tpu_custom_call" | custom-call | tf_op jit(solution)/shard_map/exchange/pallas_call | solution.py:473
  63.2 0.6 subtract_divide_fusion
Async XLA Ops:
  1.3 0.7 %copy-start.2 = (s32[256]{0:T(256)S(1)}, s32[256]{0:T(256)}, u32[]{:S(2)}) copy-start(s32[256]{0:T(256)} %param.9) | copy-start | bytes 3076
  2.0 0.8 %copy-start = (f32[64,256]{1,0:T(8,128)S(1)}, f32[64,256]{1,0:T(8,128)}, u32[]{:S(2)}) copy-start(f32[64,256]{1,0:T(8,128)} %feats_ref.1) | copy-start | bytes 196612
  2.0 0.8 %copy-start.1 = (f32[64,128]{1,0:T(8,128)S(1)}, f32[64,128]{1,0:T(8,128)}, u32[]{:S(2)}) copy-start(f32[64,128]{1,0:T(8,128)} %probes_ref.1) | copy-start | bytes 98308
